TPU v7x, 32 devices: a whole 2x2x4 slice. The times are simulated.
32 devices in a mesh: fsdp: 4 (over z), expert: 8 (over y, x, core).
Axes of the slice: x: 2, y: 2, z: 4, core: 2. Of those that a mesh axis runs over, the one named last changes fastest.
Arguments:
- tokens: bfloat16 [16384, 2048], P(('fsdp', 'expert')), may hold values from -6 to 6
- segments: int32 [32, 512], P(('fsdp', 'expert')), may hold values from 0 to 5, never falling along the last dimension, each value on 1 to 256 neighbouring positions
- routes: int32 [16384, 8], P(('fsdp', 'expert')), may hold values from 0 to 31, as said below
- w_query: bfloat16 [2048, 4096], P('fsdp'), may hold values from -0.125 to 0.125
- key_projection: bfloat16 [2048, 512], P('fsdp'), may hold values from -0.125 to 0.125
- value_projection: bfloat16 [2048, 512], P('fsdp'), may hold values from -0.125 to 0.125
- w_out: bfloat16 [4096, 2048], P('fsdp'), may hold values from -0.75 to 0.75
- w_router: bfloat16 [2048, 32], P('fsdp'), may hold values from -0.0625 to 0.0625
- gain_attn: bfloat16 [2048], P('fsdp'), may hold values from 0.5 to 1.5
- gain_ffn: bfloat16 [2048], P('fsdp'), may hold values from 0.5 to 1.5
- gain_query: bfloat16 [128], P('fsdp'), may hold values from 0.25 to 1.75
- key_head_gain: bfloat16 [128], P('fsdp'), may hold values from 0.25 to 1.75
- w_gate: bfloat16 [32, 2048, 768], P(('fsdp', 'expert')), may hold values from -0.125 to 0.125
- w_up: bfloat16 [32, 2048, 768], P(('fsdp', 'expert')), may hold values from -0.125 to 0.125
- w_down: bfloat16 [32, 768, 2048], P(('fsdp', 'expert')), may hold values from -1.25 to 1.25
- cotangent: bfloat16 [16384, 2048], P(('fsdp', 'expert')), may hold values from -6 to 6
Outputs:
- output: bfloat16 [16384, 2048], P(('fsdp', 'expert'))
- d_tokens: bfloat16 [16384, 2048], P(('fsdp', 'expert'))
- d_w_query: float32 [2048, 4096], P('fsdp')
- d_w_key: float32 [2048, 512], P('fsdp')
- d_w_value: float32 [2048, 512], P('fsdp')
- d_w_out: float32 [4096, 2048], P('fsdp')
- d_w_router: float32 [2048, 32], P('fsdp')
- d_gain_attn: float32 [2048], P('fsdp')
- d_gain_ffn: float32 [2048], P('fsdp')
- d_gain_query: float32 [128], P('fsdp')
- d_gain_key: float32 [128], P('fsdp')
- d_w_gate: float32 [32, 2048, 768], P(('fsdp', 'expert'))
- d_w_up: float32 [32, 2048, 768], P(('fsdp', 'expert'))
- d_w_down: float32 [32, 768, 2048], P(('fsdp', 'expert'))
Inputs may be any that keep to these rules, and one draw needn't show every extreme that they name: `routes`: each row names 8 different experts. In the rows of one device no expert is named more than 160 times; 8 experts, drawn from the seed, are named exactly 160 times in the rows of every device.
All inputs are finite; a program needn't handle non-finite values.
Results may differ from a plain program's by a relative error of at most 0.022.
Values may be sent and summed in bfloat16 or wider, within the bound.
A program may use at most 512 MiB of HBM per device.

v0:
```python
import jax
import jax.numpy as jnp
from jax import lax
from jax.sharding import PartitionSpec as P

MODEL_WIDTH = 2048
QUERY_HEADS = 32
KEY_VALUE_HEADS = 4
HEAD_SIZE = 128
TOP = 8
DEVICE_TOKENS = 512


EPSILON = 1e-06
ROPE_BASE = 1000000.0


def root_mean_norm(values_in, gain_in):
    return (
        values_in
        * lax.rsqrt(jnp.mean(values_in * values_in, axis=-1, keepdims=True) + EPSILON)
        * gain_in
    )


def rope_tables(sequence_length, width):
    inverse = 1.0 / ROPE_BASE ** (jnp.arange(0, width, 2, dtype=jnp.float32) / width)
    angles = jnp.arange(sequence_length, dtype=jnp.float32)[:, None] * inverse[None, :]
    angles = jnp.concatenate([angles, angles], axis=-1)
    return (jnp.cos(angles)[:, None, :], jnp.sin(angles)[:, None, :])


def rotary_apply(values_in, cosine_table, sine_values):
    half_width = values_in.shape[-1] // 2
    turned = jnp.concatenate([-values_in[..., half_width:], values_in[..., :half_width]], axis=-1)
    return values_in * cosine_table + turned * sine_values


def swiglu(gate_in, up_in):
    return jax.nn.silu(gate_in) * up_in


def route(row_block):
    return lax.all_to_all(row_block, ("fsdp", "expert"), split_axis=0, concat_axis=0, tiled=True)


def on_device(
    tokens,
    segments,
    routes,
    w_query,
    key_projection,
    value_projection,
    w_out,
    w_router,
    gain_attn,
    gain_ffn,
    gain_query,
    key_head_gain,
    w_gate,
    w_up,
    w_down,
    cotangent,
):
    gathered = (
        lax.all_gather(w_query, "fsdp", axis=0, tiled=True),
        lax.all_gather(key_projection, "fsdp", axis=0, tiled=True),
        lax.all_gather(value_projection, "fsdp", axis=0, tiled=True),
        lax.all_gather(w_out, "fsdp", axis=0, tiled=True),
        lax.all_gather(w_router, "fsdp", axis=0, tiled=True),
        lax.all_gather(gain_attn, "fsdp", axis=0, tiled=True),
        lax.all_gather(gain_ffn, "fsdp", axis=0, tiled=True),
        lax.all_gather(gain_query, "fsdp", axis=0, tiled=True),
        lax.all_gather(key_head_gain, "fsdp", axis=0, tiled=True),
    )
    (
        full_query,
        full_key,
        full_value,
        full_out,
        full_router,
        attn_gain,
        ffn_gain,
        query_gain,
        key_gain,
    ) = gathered
    sequence_length = tokens.shape[0]
    experts = lax.axis_size("fsdp") * lax.axis_size("expert")
    capacity = 5 * DEVICE_TOKENS * TOP // (4 * experts)
    query_groups = QUERY_HEADS // KEY_VALUE_HEADS
    score_scale = HEAD_SIZE ** (-0.5)
    f32 = jnp.float32
    brain_float = jnp.bfloat16
    inputs = tokens.astype(f32)
    normalized, norm_attn_back = jax.vjp(root_mean_norm, inputs, attn_gain.astype(f32))
    normed_low = normalized.astype(brain_float)
    query_raw = jnp.dot(normed_low, full_query, preferred_element_type=f32)
    key_raw = jnp.dot(normed_low, full_key, preferred_element_type=f32)
    value_reduced = jnp.dot(normed_low, full_value, preferred_element_type=f32).astype(brain_float)
    cosine_table, sine_values = rope_tables(sequence_length, HEAD_SIZE)

    def heads(query_input, key_input, gain_q, key_norm_gain):
        query_out = rotary_apply(
            root_mean_norm(query_input.reshape(sequence_length, QUERY_HEADS, HEAD_SIZE), gain_q),
            cosine_table,
            sine_values,
        )
        key_output = rotary_apply(
            root_mean_norm(
                key_input.reshape(sequence_length, KEY_VALUE_HEADS, HEAD_SIZE), key_norm_gain
            ),
            cosine_table,
            sine_values,
        )
        return (query_out, key_output)

    (query_rotated, key_rot), heads_back = jax.vjp(
        heads, query_raw, key_raw, query_gain.astype(f32), key_gain.astype(f32)
    )
    query_reduced = query_rotated.astype(brain_float).reshape(
        sequence_length, KEY_VALUE_HEADS, query_groups, HEAD_SIZE
    )
    key_low = key_rot.astype(brain_float)
    value_head_rows = value_reduced.reshape(sequence_length, KEY_VALUE_HEADS, HEAD_SIZE)
    seg_row = segments[0]
    position = jnp.arange(sequence_length)
    allowed = (seg_row[:, None] == seg_row[None, :]) & (position[None, :] <= position[:, None])

    def masked_scores():
        raw_scores = (
            jnp.einsum("sjgd,tjd->jgst", query_reduced, key_low, preferred_element_type=f32)
            * score_scale
        )
        return jnp.where(allowed, raw_scores, -1e30)

    scores = masked_scores()
    row_peak = jnp.max(scores, axis=-1, keepdims=True)
    shifted_exp = jnp.exp(scores - row_peak)
    total_weight = jnp.sum(shifted_exp, axis=-1, keepdims=True)
    attn_probs = shifted_exp / total_weight
    log_total = row_peak + jnp.log(total_weight)
    mixed_low = jnp.einsum(
        "jgst,tjd->sjgd",
        attn_probs.astype(brain_float),
        value_head_rows,
        preferred_element_type=f32,
    )
    mixed_low = mixed_low.reshape(sequence_length, QUERY_HEADS * HEAD_SIZE).astype(brain_float)
    hidden = inputs + jnp.dot(mixed_low, full_out, preferred_element_type=f32)
    routed, norm_ffn_back = jax.vjp(root_mean_norm, hidden, ffn_gain.astype(f32))
    routed_low = routed.astype(brain_float)
    logits = jnp.dot(routed_low, full_router, preferred_element_type=f32)
    expert_ids = jnp.arange(experts, dtype=jnp.int32)
    picked = (routes[:, :, None] == expert_ids[None, None, :]).astype(f32)

    def gating(logit_in):
        softmax_probs = jax.nn.softmax(logit_in, axis=-1)
        chosen = jnp.sum(softmax_probs[:, None, :] * picked, axis=-1)
        return chosen / jnp.sum(chosen, axis=-1, keepdims=True)

    gates, gating_back = jax.vjp(gating, logits)
    flat_routes = routes.reshape(-1)
    route_hits = (flat_routes[:, None] == expert_ids[None, :]).astype(jnp.int32)
    route_rank = jnp.sum((jnp.cumsum(route_hits, axis=0) - 1) * route_hits, axis=1)
    slot_place = flat_routes * capacity + route_rank
    source = (
        jnp.full((experts * capacity,), sequence_length * TOP, jnp.int32)
        .at[slot_place]
        .set(jnp.arange(sequence_length * TOP, dtype=jnp.int32))
    )
    padded_rows = jnp.concatenate([routed_low, jnp.zeros((1, MODEL_WIDTH), brain_float)], axis=0)
    send_rows = padded_rows[source // TOP].reshape(experts, capacity, MODEL_WIDTH)
    arrived = route(send_rows).reshape(experts * capacity, MODEL_WIDTH)
    gate_part = jnp.dot(arrived, w_gate[0], preferred_element_type=f32)
    up_part = jnp.dot(arrived, w_up[0], preferred_element_type=f32)
    activation, swiglu_back = jax.vjp(swiglu, gate_part, up_part)
    act_low = activation.astype(brain_float)
    expert_out = jnp.dot(act_low, w_down[0], preferred_element_type=f32).astype(brain_float)
    returned = route(expert_out.reshape(experts, capacity, MODEL_WIDTH)).reshape(
        experts * capacity, MODEL_WIDTH
    )
    picked_rows = returned[slot_place].reshape(sequence_length, TOP, MODEL_WIDTH)
    combined = hidden
    for pick_index in range(TOP):
        combined = combined + gates[:, pick_index : pick_index + 1] * picked_rows[
            :, pick_index
        ].astype(f32)
    result = combined.astype(brain_float)
    upstream = cotangent.astype(f32)
    gate_grad = jnp.stack(
        [
            jnp.sum(upstream * picked_rows[:, pick_index].astype(f32), axis=-1)
            for pick_index in range(TOP)
        ],
        axis=1,
    )
    down_grads = (
        (gates[:, :, None] * upstream[:, None, :])
        .astype(brain_float)
        .reshape(sequence_length * TOP, MODEL_WIDTH)
    )
    padded_grads = jnp.concatenate([down_grads, jnp.zeros((1, MODEL_WIDTH), brain_float)], axis=0)
    send_grads = padded_grads[source].reshape(experts, capacity, MODEL_WIDTH)
    arrived_grads = route(send_grads).reshape(experts * capacity, MODEL_WIDTH)
    act_grad = jnp.einsum("rd,fd->rf", arrived_grads, w_down[0], preferred_element_type=f32)
    down_weight_grad = jnp.einsum("rf,rd->fd", act_low, arrived_grads, preferred_element_type=f32)
    gate_part_grad, up_part_grad = swiglu_back(act_grad)
    gate_grad_low = gate_part_grad.astype(brain_float)
    up_grad_low = up_part_grad.astype(brain_float)
    gate_weight_grad = jnp.einsum("rd,rf->df", arrived, gate_grad_low, preferred_element_type=f32)
    up_weight_grad = jnp.einsum("rd,rf->df", arrived, up_grad_low, preferred_element_type=f32)
    rows_grad = (
        jnp.einsum("rf,df->rd", gate_grad_low, w_gate[0], preferred_element_type=f32)
        + jnp.einsum("rf,df->rd", up_grad_low, w_up[0], preferred_element_type=f32)
    ).astype(brain_float)
    back_rows = route(rows_grad.reshape(experts, capacity, MODEL_WIDTH)).reshape(
        experts * capacity, MODEL_WIDTH
    )
    token_grads = back_rows[slot_place].reshape(sequence_length, TOP, MODEL_WIDTH)
    routed_grad = token_grads[:, 0].astype(f32)
    for pick_index in range(1, TOP):
        routed_grad = routed_grad + token_grads[:, pick_index].astype(f32)
    logit_low = gating_back(gate_grad)[0].astype(brain_float)
    routed_grad = routed_grad + jnp.einsum(
        "se,de->sd", logit_low, full_router, preferred_element_type=f32
    )
    router_grad = jnp.einsum("sd,se->de", routed_low, logit_low, preferred_element_type=f32)
    hidden_grad, ffn_gain_grad = norm_ffn_back(routed_grad)
    hidden_grad = hidden_grad + upstream
    hidden_low = hidden_grad.astype(brain_float)
    out_grad = jnp.einsum("sa,sd->ad", mixed_low, hidden_low, preferred_element_type=f32)
    mixture_gradient = jnp.einsum(
        "sd,ad->sa", hidden_low, full_out, preferred_element_type=f32
    ).astype(brain_float)
    mixture_gradient = mixture_gradient.reshape(
        sequence_length, KEY_VALUE_HEADS, query_groups, HEAD_SIZE
    )
    scores = masked_scores()
    probs_again = jnp.exp(scores - log_total)
    probs_low = probs_again.astype(brain_float)
    prob_grad = jnp.einsum(
        "sjgd,tjd->jgst", mixture_gradient, value_head_rows, preferred_element_type=f32
    )
    value_gradient = jnp.einsum(
        "jgst,sjgd->tjd", probs_low, mixture_gradient, preferred_element_type=f32
    )
    score_grad = probs_again * (
        prob_grad - jnp.sum(prob_grad * probs_again, axis=-1, keepdims=True)
    )
    score_low = score_grad.astype(brain_float)
    query_grad = (
        jnp.einsum("jgst,tjd->sjgd", score_low, key_low, preferred_element_type=f32) * score_scale
    )
    key_grad = (
        jnp.einsum("jgst,sjgd->tjd", score_low, query_reduced, preferred_element_type=f32)
        * score_scale
    )
    query_pre, key_pre, query_gain_grad, key_gain_grad = heads_back(
        (query_grad.reshape(sequence_length, QUERY_HEADS, HEAD_SIZE), key_grad)
    )
    query_pre_low = query_pre.astype(brain_float)
    key_pre_low = key_pre.astype(brain_float)
    value_before_reduced = value_gradient.reshape(
        sequence_length, KEY_VALUE_HEADS * HEAD_SIZE
    ).astype(brain_float)
    query_weight_grad = jnp.einsum(
        "sd,sa->da", normed_low, query_pre_low, preferred_element_type=f32
    )
    key_weight_grad = jnp.einsum("sd,sa->da", normed_low, key_pre_low, preferred_element_type=f32)
    value_weight_grad = jnp.einsum(
        "sd,sa->da", normed_low, value_before_reduced, preferred_element_type=f32
    )
    normed_grad = (
        jnp.einsum("sa,da->sd", query_pre_low, full_query, preferred_element_type=f32)
        + jnp.einsum("sa,da->sd", key_pre_low, full_key, preferred_element_type=f32)
        + jnp.einsum("sa,da->sd", value_before_reduced, full_value, preferred_element_type=f32)
    )
    input_grad, attn_gain_grad = norm_attn_back(normed_grad)
    input_grad = (input_grad + hidden_grad).astype(brain_float)
    local_grads = (
        query_weight_grad,
        key_weight_grad,
        value_weight_grad,
        out_grad,
        router_grad,
        attn_gain_grad,
        ffn_gain_grad,
        query_gain_grad,
        key_gain_grad,
    )
    shard_sums = (
        lax.psum_scatter(
            local_grads[0].astype(jnp.bfloat16), "fsdp", scatter_dimension=0, tiled=True
        ).astype(jnp.float32),
        lax.psum_scatter(
            local_grads[1].astype(jnp.bfloat16), "fsdp", scatter_dimension=0, tiled=True
        ).astype(jnp.float32),
        lax.psum_scatter(
            local_grads[2].astype(jnp.bfloat16), "fsdp", scatter_dimension=0, tiled=True
        ).astype(jnp.float32),
        lax.psum_scatter(
            local_grads[3].astype(jnp.bfloat16), "fsdp", scatter_dimension=0, tiled=True
        ).astype(jnp.float32),
        lax.psum_scatter(
            local_grads[4].astype(jnp.bfloat16), "fsdp", scatter_dimension=0, tiled=True
        ).astype(jnp.float32),
        lax.psum_scatter(
            local_grads[5].astype(jnp.bfloat16), "fsdp", scatter_dimension=0, tiled=True
        ).astype(jnp.float32),
        lax.psum_scatter(
            local_grads[6].astype(jnp.bfloat16), "fsdp", scatter_dimension=0, tiled=True
        ).astype(jnp.float32),
        lax.psum_scatter(
            local_grads[7].astype(jnp.bfloat16), "fsdp", scatter_dimension=0, tiled=True
        ).astype(jnp.float32),
        lax.psum_scatter(
            local_grads[8].astype(jnp.bfloat16), "fsdp", scatter_dimension=0, tiled=True
        ).astype(jnp.float32),
    )
    summed = (
        lax.psum(shard_sums[0].astype(jnp.bfloat16), "expert").astype(jnp.float32),
        lax.psum(shard_sums[1].astype(jnp.bfloat16), "expert").astype(jnp.float32),
        lax.psum(shard_sums[2].astype(jnp.bfloat16), "expert").astype(jnp.float32),
        lax.psum(shard_sums[3].astype(jnp.bfloat16), "expert").astype(jnp.float32),
        lax.psum(shard_sums[4].astype(jnp.bfloat16), "expert").astype(jnp.float32),
        lax.psum(shard_sums[5].astype(jnp.bfloat16), "expert").astype(jnp.float32),
        lax.psum(shard_sums[6].astype(jnp.bfloat16), "expert").astype(jnp.float32),
        lax.psum(shard_sums[7].astype(jnp.bfloat16), "expert").astype(jnp.float32),
        lax.psum(shard_sums[8].astype(jnp.bfloat16), "expert").astype(jnp.float32),
    )
    return (
        (result, input_grad)
        + tuple(summed)
        + (gate_weight_grad[None], up_weight_grad[None], down_weight_grad[None])
    )


def solution(mesh):
    in_specs = (
        P(("fsdp", "expert"), None),
        P(("fsdp", "expert"), None),
        P(("fsdp", "expert"), None),
        P("fsdp", None),
        P("fsdp", None),
        P("fsdp", None),
        P("fsdp", None),
        P("fsdp", None),
        P("fsdp"),
        P("fsdp"),
        P("fsdp"),
        P("fsdp"),
        P(("fsdp", "expert"), None, None),
        P(("fsdp", "expert"), None, None),
        P(("fsdp", "expert"), None, None),
        P(("fsdp", "expert"), None),
    )
    out_specs = (
        P(("fsdp", "expert"), None),
        P(("fsdp", "expert"), None),
        P("fsdp", None),
        P("fsdp", None),
        P("fsdp", None),
        P("fsdp", None),
        P("fsdp", None),
        P("fsdp"),
        P("fsdp"),
        P("fsdp"),
        P("fsdp"),
        P(("fsdp", "expert"), None, None),
        P(("fsdp", "expert"), None, None),
        P(("fsdp", "expert"), None, None),
    )
    return jax.shard_map(
        on_device, mesh=mesh, in_specs=in_specs, out_specs=out_specs, check_vma=False
    )
```

profile of v0, /device:TPU:11, one launch (start us, length us, event | category | flops | bytes accessed | tf_op | source)
XLA Modules:
  0.0 3822.5 jit_solution(12137805447198674976)
XLA Ops:
  40.5 18.1 reduce-window.6
  62.3 15.8 scatter_custom_fusion
  89.3 12.1 all-gather.7.cloned.1.call-done
  105.9 281.8 %all-gather.11.cloned.1.call-done = bf16[2048,4096]{1,0:T(8,128)(2,1)} async-done(((bf16[512,4096]{1,0:T(8,128)(2,1)}), bf16[2048,4096]{1,0:T(8,128)(2,1)}) %all-gather.11.cloned.1.call-update) | async-done | bytes 16777232 | tf_op jit(solution)/shard_map/all_gather | solution.py:66
  387.7 16.0 multiply_reduce_fusion.2
  419.9 14.1 fusion.11
  434.0 14.6 fusion.4
  448.7 16.9 fusion.54
  465.6 208.5 %all-gather.13.cloned.1.call-done = bf16[4096,2048]{1,0:T(8,128)(2,1)} async-done(((bf16[1024,2048]{1,0:T(8,128)(2,1)}), bf16[4096,2048]{1,0:T(8,128)(2,1)}) %all-gather.13.cloned.1.call-update) | async-done | bytes 16777232 | tf_op jit(solution)/shard_map/all_gather | solution.py:69
  674.1 14.3 multiply_reduce_fusion.5
  691.9 40.7 %gather_fusion = bf16[5120,2048]{1,0:T(8,128)(2,1)} fusion(bf16[513,2048]{1,0:T(8,128)(2,1)} %concatenate.33, s32[5120]{0:T(1024)S(1)} %copy-done.61), kind=kCustom, calls=%fused_computation | custom fusion | bytes 41963520 | tf_op jit(solution)/shard_map/gather | solution.py:172
  744.2 452.6 %all_gather.35 = bf16[2048,32]{0,1:T(8,128)(2,1)S(1)} all-gather(bf16[512,32]{0,1:T(8,128)(2,1)S(1)} %copy-done.72), channel_id=1, replica_groups=mesh['fsdp'=4,'expert'=8] {'fsdp'}, dimensions={0}, use_global_device_ids=true | all-gather | bytes 163840 | tf_op jit(solution)/shard_map/all_gather | solution.py:70
  1213.9 46.8 %gather_fusion.2 = bf16[5120,2048]{1,0:T(8,128)(2,1)} fusion(bf16[4097,2048]{1,0:T(8,128)(2,1)} %concatenate.34, s32[5120]{0:T(1024)S(1)} %copy-done.60), kind=kCustom, calls=%fused_computation.2 | custom fusion | bytes 41963520 | tf_op jit(solution)/shard_map/gather | solution.py:203
  1260.7 20.2 all-to-all-start.2
  1281.0 23.2 fusion.48
  1304.2 22.2 fusion.52
  1326.4 406.6 %all-to-all-done.2 = bf16[32,160,2048]{2,1,0:T(8,128)(2,1)} async-done(((bf16[32,160,2048]{2,1,0:T(8,128)(2,1)}), bf16[32,160,2048]{2,1,0:T(8,128)(2,1)}, u32[]{:S(2)}, u32[]{:S(2)}) %all-to-all-start.2) | async-done | bytes 20971552 | tf_op jit(solution)/shard_map/all_to_all | solution.py:44
  1733.0 32.3 multiply_convert_fusion
  1765.3 22.8 convolution_convert_fusion
  1788.0 19.2 all-to-all-start.1
  1807.2 24.5 fusion.50
  1831.8 29.8 add_convert_fusion
  1861.5 397.7 %all-to-all-done.1 = bf16[32,160,2048]{2,1,0:T(8,128)(2,1)} async-done(((bf16[32,160,2048]{2,1,0:T(8,128)(2,1)}), bf16[32,160,2048]{2,1,0:T(8,128)(2,1)}, u32[]{:S(2)}, u32[]{:S(2)}) %all-to-all-start.1) | async-done | bytes 20971552 | tf_op jit(solution)/shard_map/all_to_all | solution.py:44
  2259.3 19.0 all-to-all-start.3
  2279.1 41.2 %gather_fusion.1 = bf16[4096,2048]{1,0:T(8,128)(2,1)} fusion(bf16[5120,2048]{1,0:T(8,128)(2,1)} %bitcast.27, s32[4096]{0:T(1024)S(1)} %broadcast_clamp_fusion), kind=kCustom, calls=%fused_computation.1 | custom fusion | bytes 33570816 | tf_op jit(solution)/shard_map/gather | solution.py:182
  2320.3 74.0 %fusion.94 = (bf16[512,1,2048]{2,1,0:T(2,128)(2,1)}, bf16[512,1,2048]{2,1,0:T(2,128)(2,1)}, bf16[512,1,2048]{2,1,0:T(2,128)(2,1)}, bf16[512,1,2048]{2,1,0:T(2,12...) fusion(bf16[512,8,2048]{2,1,0:T(8,128)(2,1)} %bitcast.271), kind=kLoop, calls=%fused_computation.218 | loop fusion | bytes 33554432 | tf_op jit(solution)/shard_map/slice | solution.py:185
  2394.4 26.2 fusion.41
  2420.9 309.6 %all-to-all-done.3 = bf16[32,160,2048]{2,1,0:T(8,128)(2,1)} async-done(((bf16[32,160,2048]{2,1,0:T(8,128)(2,1)}), bf16[32,160,2048]{2,1,0:T(8,128)(2,1)}, u32[]{:S(2)}, u32[]{:S(2)}) %all-to-all-start.3) | async-done | bytes 20971552 | tf_op jit(solution)/shard_map/all_to_all | solution.py:44
  2730.5 41.0 %gather_fusion.3 = bf16[4096,2048]{1,0:T(8,128)(2,1)} fusion(bf16[5120,2048]{1,0:T(8,128)(2,1)} %bitcast.51, s32[4096]{0:T(1024)S(1)} %broadcast_clamp_fusion), kind=kCustom, calls=%fused_computation.3 | custom fusion | bytes 33570816 | tf_op jit(solution)/shard_map/gather | solution.py:219
  2771.5 74.0 %fusion.93 = (bf16[512,1,2048]{2,1,0:T(2,128)(2,1)}, bf16[512,1,2048]{2,1,0:T(2,128)(2,1)}, bf16[512,1,2048]{2,1,0:T(2,128)(2,1)}, bf16[512,1,2048]{2,1,0:T(2,12...) fusion(bf16[512,8,2048]{2,1,0:T(8,128)(2,1)} %bitcast.270), kind=kLoop, calls=%fused_computation.217 | loop fusion | bytes 33554432 | tf_op jit(solution)/shard_map/slice | solution.py:220
  2845.6 25.8 multiply_reduce_fusion.3
  2874.6 13.9 fusion.55
  2889.8 25.9 fusion
  2915.8 34.4 fusion.2
  2950.2 13.5 broadcast_multiply_fusion.1
  2970.2 28.7 copy.193
  3010.8 15.7 convolution_convert_fusion.1
  3044.3 16.4 multiply_reduce_fusion
  3069.5 15.1 convolution_convert_fusion.2
  3086.0 23.5 convolution_bitcast_fusion
  3110.7 23.2 convolution_bitcast_fusion.1
  3133.9 215.1 %reduce-scatter.12.cloned.1.call-done = bf16[1024,2048]{1,0:T(8,128)(2,1)} async-done(((bf16[4096,2048]{1,0:T(8,128)(2,1)}), bf16[1024,2048]{1,0:T(8,128)(2,1)}) %reduce-scatter.12.cloned.1.call-update) | async-done | bytes 4194320 | tf_op jit(solution)/shard_map/reduce_scatter | solution.py:301
  3349.0 283.5 %reduce-scatter.6.cloned.1.call-done = bf16[512,4096]{1,0:T(8,128)(2,1)} async-done(((bf16[2048,4096]{1,0:T(8,128)(2,1)}), bf16[512,4096]{1,0:T(8,128)(2,1)}) %reduce-scatter.6.cloned.1.call-update) | async-done | bytes 4194320 | tf_op jit(solution)/shard_map/reduce_scatter | solution.py:292
  3632.6 23.1 convolution_bitcast_fusion.2
  3662.4 18.9 fusion.20
  3681.3 10.8 all-reduce.14
  3698.5 24.7 all-reduce.12
  3726.0 73.6 %all-reduce.18.cloned.1.call-done = (bf16[512,4096]{1,0:T(8,128)(2,1)}, bf16[512,512]{1,0:T(8,128)(2,1)}, bf16[512,512]{1,0:T(8,128)(2,1)}, bf16[1024,2048]{1,0:T(8,128)(2,1)}) async-done(((bf16[512,4096]{1,0:T(8,128)(2,1)}, bf16[512,512]{1,0:T(8,128)(2,1)}, bf16[512,512]{1,0:T(8,128)(2,1)}, bf16[1024,2048]{1,0:T(8,128)(2,1)}), (bf16[512,4096]{1,0:T(8,128)(2,1)}, bf16[512,512]{1,0:T(8,128)(2,1)}, ...) | async-done | bytes 9437200 | tf_op jit(solution)/shard_map/psum | solution.py:321
  (332 shorter events, 182.9 us)
Async XLA Ops:
  7.2 1725.8 %copy-start = (bf16[1,768,2048]{2,1,0:T(8,128)(2,1)S(1)}, bf16[1,768,2048]{2,1,0:T(8,128)(2,1)}, u32[]{:S(2)}) copy-start(bf16[1,768,2048]{2,1,0:T(8,128)(2,1)} %param.30) | copy-start | bytes 9437188
  7.2 75.8 %all-gather.9.cloned.1.call-start = ((), (), s32[]{:S(2)}) async-start(), calls=%async_computation.10 | async-start | bytes 2621440 | tf_op jit(solution)/shard_map/all_gather | solution.py:67
  7.9 93.5 %all-gather.7.cloned.1.call-start = ((), (), s32[]{:S(2)}) async-start(), calls=%async_computation.9 | async-start | bytes 2621440 | tf_op jit(solution)/shard_map/all_gather | solution.py:68
  8.7 378.9 %all-gather.11.cloned.1.call-start = ((), (), s32[]{:S(2)}) async-start(), calls=%async_computation.11 | async-start | bytes 20971520 | tf_op jit(solution)/shard_map/all_gather | solution.py:66
  9.5 664.6 %all-gather.13.cloned.1.call-start = ((), (), s32[]{:S(2)}) async-start(), calls=%async_computation.12 | async-start | bytes 20971520 | tf_op jit(solution)/shard_map/all_gather | solution.py:69
  10.4 72.3 %copy-start.83 = (s32[1,512]{1,0:T(1,128)S(1)}, s32[1,512]{1,0:T(1,128)}, u32[]{:S(2)}) copy-start(s32[1,512]{1,0:T(1,128)} %param.17) | copy-start | bytes 6148
  19.6 67.5 %copy-start.88 = (f32[128]{0:T(128)}, f32[128]{0:T(128)S(1)}, u32[]{:S(2)}) copy-start(f32[128]{0:T(128)S(1)} %convert_element_type.285) | copy-start | bytes 1540
  19.6 395.4 %copy-start.81 = (f32[128]{0:T(128)}, f32[128]{0:T(128)S(1)}, u32[]{:S(2)}) copy-start(f32[128]{0:T(128)S(1)} %convert_element_type.287) | copy-start | bytes 1540
  29.7 658.7 %copy-start.62 = (f32[4,1,512]{2,1,0:T(1,128)}, f32[4,1,512]{2,1,0:T(1,128)S(1)}, u32[]{:S(2)}) copy-start(f32[4,1,512]{2,1,0:T(1,128)S(1)} %convert_element_type.376) | copy-start | bytes 24580
  39.3 348.3 %copy-start.70 = (f32[4,1,512]{2,1,0:T(1,128)}, f32[4,1,512]{2,1,0:T(1,128)S(1)}, u32[]{:S(2)}) copy-start(f32[4,1,512]{2,1,0:T(1,128)S(1)} %convert_element_type.375) | copy-start | bytes 24580
  62.2 24.4 copy-start.64
  82.1 305.6 %copy-start.84 = (f32[512]{0:T(512)}, f32[512]{0:T(512)S(1)}, u32[]{:S(2)}) copy-start(f32[512]{0:T(512)S(1)} %fusion.80) | copy-start | bytes 6148
  82.9 365.8 %copy-start.11 = (pred[512,512]{0,1:T(8,128)(4,1)}, pred[512,512]{0,1:T(8,128)(4,1)S(1)}, u32[]{:S(2)}) copy-start(pred[512,512]{0,1:T(8,128)(4,1)S(1)} %fusion.62) | copy-start | bytes 786436
  86.7 19.2 copy-start.75
  732.7 528.1 %all-to-all-start = ((bf16[32,160,2048]{2,1,0:T(8,128)(2,1)}), bf16[32,160,2048]{2,1,0:T(8,128)(2,1)}, u32[]{:S(2)}, u32[]{:S(2)}) async-start(bf16[32,160,2048]{2,1,0:T(8,128)(2,1)} %bitcast.272), calls=%async_computation | async-start | bytes 41943040 | tf_op jit(solution)/shard_map/all_to_all | solution.py:44
  739.9 456.9 %copy-start.9 = (bf16[512,2048]{1,0:T(8,128)(2,1)S(1)}, bf16[512,2048]{1,0:T(8,128)(2,1)}, u32[]{:S(2)}) copy-start(bf16[512,2048]{1,0:T(8,128)(2,1)} %copy-done.8) | copy-start | bytes 6291460
  739.9 458.9 %copy-start.50 = (s32[512,8]{0,1:T(8,128)S(1)}, s32[512,8]{0,1:T(8,128)}, u32[]{:S(2)}) copy-start(s32[512,8]{0,1:T(8,128)} %param.18) | copy-start | bytes 49156
  1260.7 472.3 %all-to-all-start.2 = ((bf16[32,160,2048]{2,1,0:T(8,128)(2,1)}), bf16[32,160,2048]{2,1,0:T(8,128)(2,1)}, u32[]{:S(2)}, u32[]{:S(2)}) async-start(bf16[32,160,2048]{2,1,0:T(8,128)(2,1)} %bitcast.273), calls=%async_computation.2 | async-start | bytes 41943040 | tf_op jit(solution)/shard_map/all_to_all | solution.py:44
  1281.0 23.3 copy-start.95
  1788.0 19.2 copy-start.96
  1788.0 471.2 %all-to-all-start.1 = ((bf16[32,160,2048]{2,1,0:T(8,128)(2,1)}), bf16[32,160,2048]{2,1,0:T(8,128)(2,1)}, u32[]{:S(2)}, u32[]{:S(2)}) async-start(bf16[32,160,2048]{2,1,0:T(8,128)(2,1)} %bitcast.278), calls=%async_computation.1 | async-start | bytes 41943040 | tf_op jit(solution)/shard_map/all_to_all | solution.py:44
  2259.3 19.2 copy-start.46
  2259.3 471.2 %all-to-all-start.3 = ((bf16[32,160,2048]{2,1,0:T(8,128)(2,1)}), bf16[32,160,2048]{2,1,0:T(8,128)(2,1)}, u32[]{:S(2)}, u32[]{:S(2)}) async-start(bf16[32,160,2048]{2,1,0:T(8,128)(2,1)} %bitcast.277), calls=%async_computation.3 | async-start | bytes 41943040 | tf_op jit(solution)/shard_map/all_to_all | solution.py:44
  2278.3 855.7 %reduce-scatter.8.cloned.1.call-start = ((), (), s32[]{:S(2)}) async-start(), calls=%async_computation.14 | async-start | bytes 2621440 | tf_op jit(solution)/shard_map/reduce_scatter | solution.py:295
  2320.3 74.0 %copy-start.4 = (f32[512,2048]{1,0:T(8,128)S(1)}, f32[512,2048]{1,0:T(8,128)}, u32[]{:S(2)}) copy-start(f32[512,2048]{1,0:T(8,128)} %copy-done.3) | copy-start | bytes 12582916
  2320.3 74.0 %copy-start.15 = (bf16[512,2048]{1,0:T(8,128)(2,1)S(1)}, bf16[512,2048]{1,0:T(8,128)(2,1)}, u32[]{:S(2)}) copy-start(bf16[512,2048]{1,0:T(8,128)(2,1)} %param.31) | copy-start | bytes 6291460
  2394.3 26.3 copy-start.55
  2394.3 26.3 copy-start.51
  2394.4 26.4 copy-start.35
  2394.4 26.4 copy-start.67
  2420.8 424.7 %copy-start.58 = (bf16[512,32]{0,1:T(8,128)(2,1)}, bf16[512,32]{0,1:T(8,128)(2,1)S(1)}, u32[]{:S(2)}) copy-start(bf16[512,32]{0,1:T(8,128)(2,1)S(1)} %multiply_convert_fusion.3) | copy-start | bytes 98308
  2771.5 74.1 %copy-start.5 = (f32[512,2048]{1,0:T(8,128)S(1)}, f32[512,2048]{1,0:T(8,128)}, u32[]{:S(2)}) copy-start(f32[512,2048]{1,0:T(8,128)} %copy-done.3) | copy-start | bytes 12582916
  2771.5 74.1 %copy-start.44 = (bf16[2048,32]{0,1:T(8,128)(2,1)S(1)}, bf16[2048,32]{0,1:T(8,128)(2,1)}, u32[]{:S(2)}) copy-start(bf16[2048,32]{0,1:T(8,128)(2,1)} %copy-done.43) | copy-start | bytes 393220
  2771.5 74.1 %copy-start.63 = (f32[4,1,512]{2,1,0:T(1,128)S(1)}, f32[4,1,512]{2,1,0:T(1,128)}, u32[]{:S(2)}) copy-start(f32[4,1,512]{2,1,0:T(1,128)} %copy-done.62) | copy-start | bytes 24580
  2771.5 74.1 %copy-start.80 = (f32[512]{0:T(512)S(1)}, f32[512]{0:T(512)}, u32[]{:S(2)}) copy-start(f32[512]{0:T(512)} %copy-done.79) | copy-start | bytes 6148
  2845.6 25.8 copy-start.87
  2889.8 26.0 copy-start.6
  2915.8 34.4 copy-start.18
  2970.2 163.7 %reduce-scatter.10.cloned.1.call-start = ((), (), s32[]{:S(2)}) async-start(), calls=%async_computation.15 | async-start | bytes 2621440 | tf_op jit(solution)/shard_map/reduce_scatter | solution.py:298
  3010.8 338.2 %reduce-scatter.12.cloned.1.call-start = ((), (), s32[]{:S(2)}) async-start(), calls=%async_computation.16 | async-start | bytes 20971520 | tf_op jit(solution)/shard_map/reduce_scatter | solution.py:301
  3026.6 606.0 %reduce-scatter.6.cloned.1.call-start = ((), (), s32[]{:S(2)}) async-start(), calls=%async_computation.13 | async-start | bytes 20971520 | tf_op jit(solution)/shard_map/reduce_scatter | solution.py:292
  3084.6 613.9 %reduce-scatter.14.cloned.1.call-start = ((), (), s32[]{:S(2)}) async-start(), calls=%async_computation.17 | async-start | bytes 163840 | tf_op jit(solution)/shard_map/reduce_scatter | solution.py:304
  3085.9 23.6 copy-start.10
  3086.0 23.6 copy-start.59
  3110.6 689.0 %all-reduce.18.cloned.1.call-start = ((), (), s32[]{:S(2)}) async-start(), calls=%async_computation.18 | async-start | bytes 18874368 | tf_op jit(solution)/shard_map/psum | solution.py:321
  3632.5 23.1 copy-start.29
  3632.6 23.1 copy-start.32
  3662.4 30.1 copy-start.78
  (67 other events, 437.9 us)
Sparse Core Ops, SparseCore 0:
  9.6 45.5 all-gather.8
  56.8 44.5 all-gather.6
  103.0 284.5 all-gather.10
  389.1 284.9 all-gather.12
  2970.3 51.7 reduce-scatter.7
  3024.3 43.1 reduce-scatter.9
  3069.9 279.0 reduce-scatter.11
  3351.5 281.0 reduce-scatter.5
  3634.8 18.3 reduce-scatter.13
  3657.5 142.0 all-reduce.17
where the time goes:
time: 3830 us; the launch traced here: 3820 us
  waiting for transfers between devices  2190 us (57%)
  blocking collectives  515 us (13%)
  matrix products  454 us (12%)
  local copies, waits for them, and re-layouts  385 us (10%)
  other arithmetic  193 us (5%)
  starting transfers between devices  66 us (2%)
    all_to_all x4, waiting for transfers between devices, route(): lax.all_to_all(row_block, ('fsdp', 'expert'), split_axis=0, concat_axis=0...  1110 us
    all_gather x1, blocking collectives, on_device(): lax.all_gather(w_router, 'fsdp', axis=0, tiled=True)  453 us
    reduce_scatter x1, waiting for transfers between devices, on_device(): lax.psum_scatter(local_grads[0].astype(jnp.bfloat16), 'fsdp', scatter_dim...  284 us
    all_gather x1, waiting for transfers between devices, on_device(): lax.all_gather(w_query, 'fsdp', axis=0, tiled=True)  282 us
    reduce_scatter x1, waiting for transfers between devices, on_device(): lax.psum_scatter(local_grads[3].astype(jnp.bfloat16), 'fsdp', scatter_dim...  215 us
    all_gather x1, waiting for transfers between devices, on_device(): lax.all_gather(w_out, 'fsdp', axis=0, tiled=True)  208 us
  transfers between devices with their start and end apart: 14, of which 9 were waited for; matrix products, arithmetic and copies ran while one was open for 17% of the time, Pallas kernels for 0%

commit v1 on v0

v1 whole, which is shorter than its diff:
```python
import functools

import jax
import jax.numpy as jnp
from jax import lax
from jax.experimental import pallas as pl
from jax.experimental.pallas import tpu as pltpu
from jax.sharding import PartitionSpec as P

MODEL_WIDTH = 2048
QUERY_HEADS = 32
KEY_VALUE_HEADS = 4
HEAD_SIZE = 128
TOP = 8
DEVICE_TOKENS = 512


EPSILON = 1e-06
ROPE_BASE = 1000000.0


def root_mean_norm(values_in, gain_in):
    return (
        values_in
        * lax.rsqrt(jnp.mean(values_in * values_in, axis=-1, keepdims=True) + EPSILON)
        * gain_in
    )


def rope_tables(sequence_length, width):
    inverse = 1.0 / ROPE_BASE ** (jnp.arange(0, width, 2, dtype=jnp.float32) / width)
    angles = jnp.arange(sequence_length, dtype=jnp.float32)[:, None] * inverse[None, :]
    cosine, sine = jnp.cos(angles), jnp.sin(angles)
    return (
        jnp.concatenate([cosine, cosine], axis=-1),
        jnp.concatenate([-sine, sine], axis=-1),
    )


def swiglu(gate_in, up_in):
    return jax.nn.silu(gate_in) * up_in


BOTH = ("fsdp", "expert")


def gather_shards(shard):
    parts = lax.axis_size("expert")
    rows = shard.shape[0] // parts
    own = lax.dynamic_slice_in_dim(shard, lax.axis_index("expert") * rows, rows, axis=0)
    return lax.all_gather(own, BOTH, axis=0, tiled=True)


def scatter_sums(whole):
    part = lax.psum_scatter(whole, BOTH, scatter_dimension=0, tiled=True)
    return lax.all_gather(part, "expert", axis=0, tiled=True).astype(jnp.float32)


def routed_weight_grads(rows, gate_low, up_low):
    return tuple(
        jnp.einsum("rd,rf->df", rows, low, preferred_element_type=jnp.float32)
        for low in (gate_low, up_low)
    )


def down_weight_grads(row_cotangent, act_scaled):
    return jnp.einsum(
        "rf,rd->fd", act_scaled, row_cotangent, preferred_element_type=jnp.float32
    )


def expert_layer(rows, row_cotangent, row_gates, w_gate, w_up, w_down):
    f32 = jnp.float32
    low = jnp.bfloat16
    gate_part = jnp.dot(rows, w_gate, preferred_element_type=f32)
    up_part = jnp.dot(rows, w_up, preferred_element_type=f32)
    activation, swiglu_back = jax.vjp(swiglu, gate_part, up_part)
    act_low = activation.astype(low)
    out_rows = (
        jnp.dot(act_low, w_down, preferred_element_type=f32) * row_gates[:, None]
    ).astype(low)
    act_pull = jnp.einsum("rd,fd->rf", row_cotangent, w_down, preferred_element_type=f32)
    gate_grad = jnp.sum(act_low.astype(f32) * act_pull, axis=-1)
    act_scaled = (act_low.astype(f32) * row_gates[:, None]).astype(low)
    gate_part_grad, up_part_grad = swiglu_back(act_pull * row_gates[:, None])
    gate_low = gate_part_grad.astype(low)
    up_low = up_part_grad.astype(low)
    rows_grad = (
        jnp.einsum("rf,df->rd", gate_low, w_gate, preferred_element_type=f32)
        + jnp.einsum("rf,df->rd", up_low, w_up, preferred_element_type=f32)
    ).astype(low)
    weight_grads = routed_weight_grads(rows, gate_low, up_low)
    weight_grads += (down_weight_grads(row_cotangent, act_scaled),)
    return (out_rows, rows_grad, gate_grad) + weight_grads


def ranks(hits):
    length = hits.shape[-1]
    before = jnp.arange(length)[:, None] <= jnp.arange(length)[None, :]
    counts = jnp.einsum(
        "...s,st->...t",
        hits.astype(jnp.bfloat16),
        before.astype(jnp.bfloat16),
        preferred_element_type=jnp.float32,
    )
    return jnp.where(hits, counts.astype(jnp.int32) - 1, -1)


def places(hits, capacity):
    slots = jnp.arange(capacity, dtype=jnp.int32)
    return (ranks(hits)[..., None, :] == slots[:, None]).astype(jnp.bfloat16)


MESH = pl.DeviceIdType.MESH
LINE = 4
PLANE = 8
PART = 512
FAR_FIRST = (3, 0, 2, 1)


class Place:
    def __init__(self):
        self.z = lax.axis_index("fsdp")
        self.e = lax.axis_index("expert")
        core = lax.rem(self.e, 2)
        x = lax.rem(lax.div(self.e, 2), 2)
        y = lax.div(self.e, 4)
        self.sib = self.e + 1 - 2 * core
        self.x_same = self.e + 2 - 4 * x
        self.y_same = self.e + 4 - 8 * y
        self.d_same = self.x_same + 4 - 8 * y
        self.x_other = self.x_same + 1 - 2 * core
        self.y_other = self.y_same + 1 - 2 * core
        self.d_other = self.d_same + 1 - 2 * core
        self.plane = [lax.rem(self.e + k, PLANE) for k in range(1, PLANE)]
        self.line = [lax.rem(self.z + k, LINE) for k in range(1, LINE)]

    def greet(self):
        barrier = pltpu.get_barrier_semaphore()
        others = [(self.z, other) for other in self.plane] + [(other, self.e) for other in self.line]
        for z, e in others:
            pl.semaphore_signal(barrier, inc=1, device_id=(z, e), device_id_type=MESH)
        pl.semaphore_wait(barrier, len(others))


def push(source, target, send, recv, z, e):
    return pltpu.make_async_remote_copy(
        src_ref=source,
        dst_ref=target,
        send_sem=send,
        recv_sem=recv,
        device_id=(z, e),
        device_id_type=MESH,
    )


def part_columns(half, part):
    return pl.ds(half * 2 * PART + part * PART, PART)


def one_hot(pos_ref, experts, block, capacity):
    slots = lax.broadcasted_iota(jnp.int32, (capacity, DEVICE_TOKENS), 0)
    return jnp.concatenate(
        [
            (slots == pos_ref[expert, pl.ds(block, 1), :]).astype(jnp.float32)
            for expert in experts
        ],
        axis=0,
    ).astype(jnp.bfloat16)


def along_line(here, source, goal, send, recv):
    return [
        push(
            source.at[plane],
            goal.at[here.z],
            send.at[k],
            recv.at[here.z],
            plane,
            here.e,
        )
        for k, plane in enumerate(here.line)
    ]


def in_plane_of(here, source, goal, send, recv):
    return [
        push(
            source.at[:, owner],
            goal.at[:, here.e],
            send.at[k],
            recv.at[here.e],
            here.z,
            owner,
        )
        for k, owner in enumerate(here.plane)
    ]


def target_sets(here):
    with_y = (here.e, here.sib, here.y_same, here.y_other)
    with_x = (here.e, here.sib, here.x_same, here.x_other)
    return (
        (here.e, 0, with_y),
        (here.e, 1, with_x),
        (here.x_same, 0, with_y),
        (here.y_same, 1, with_x),
    )


CUTS = 4
CUT = 256
AHEAD = 2


def cut_columns(half, part):
    return pl.ds(half * CUTS * CUT + part * CUT, CUT)


def combine_kernel(
    pos_ref,
    gate_grad_ref,
    rows_ref,
    out_ref,
    gate_out_ref,
    gates_plane,
    held,
    dense_out,
    dense_in,
    sums,
    passed,
    held_send,
    held_recv,
    dense_send,
    dense_recv,
    pass_send,
    pass_recv,
    gate_plane_send,
    gate_plane_recv,
    gate_line_send,
    gate_line_recv,
):
    here = Place()
    z, e = here.z, here.e
    capacity = rows_ref.shape[1]
    here.greet()
    targets = target_sets(here)
    units = [(part, plane) for part in range(CUTS) for plane in FAR_FIRST]
    at_end = []

    def unit_of(part, plane):
        return part * LINE + plane

    def compact(index):
        part, plane = units[index]
        unit = unit_of(part, plane)

        def rows_of(owner, half):
            return rows_ref.at[plane * PLANE + owner, :, cut_columns(half, part)]

        def slot(number, k):
            return held.at[unit, number, pl.ds(k * capacity, capacity)]

        for number, owner, half in (
            (2, here.x_same, 0),
            (3, here.y_same, 1),
            (0, here.e, 0),
            (1, here.e, 1),
        ):
            pltpu.make_async_copy(
                rows_of(owner, half), slot(number, 0), held_recv.at[unit, number, 0]
            ).start()
        for count, (goal, number, k, owner, half) in enumerate(
            (
                (here.y_same, 2, 2, here.d_same, 0),
                (here.x_same, 3, 2, here.d_same, 1),
                (here.y_other, 2, 3, here.d_other, 0),
                (here.x_other, 3, 3, here.d_other, 1),
                (here.sib, 2, 1, here.x_other, 0),
                (here.sib, 3, 1, here.y_other, 1),
                (here.sib, 0, 1, here.sib, 0),
                (here.sib, 1, 1, here.sib, 1),
                (here.y_same, 0, 2, here.y_same, 0),
                (here.x_same, 1, 2, here.x_same, 1),
                (here.y_other, 0, 3, here.y_other, 0),
                (here.x_other, 1, 3, here.x_other, 1),
            )
        ):
            send = push(
                rows_of(owner, half),
                slot(number, k),
                held_send.at[unit, count],
                held_recv.at[unit, number, k],
                z,
                goal,
            )
            send.start()
            at_end.append((None, [send]))

    def put_together(index, number):
        part, plane = units[index]
        unit = unit_of(part, plane)
        owner, _, experts = targets[number]
        for k in range(4):
            wait_for(
                held.at[unit, number, pl.ds(k * capacity, capacity)],
                held_recv.at[unit, number, k],
            )
        select = one_hot(pos_ref, experts, plane * PLANE + owner, capacity)
        return lax.dot_general(
            select,
            held[unit, number],
            (((0,), (0,)), ((), ())),
            preferred_element_type=jnp.float32,
        )

    def first(index):
        part, plane = units[index]
        unit = unit_of(part, plane)
        slot = index % 4
        for half in range(2):
            send = push(
                dense_out.at[half, slot],
                dense_in.at[half, unit],
                dense_send.at[half, slot],
                dense_recv.at[half, unit],
                z,
                (here.x_same, here.y_same)[half],
            )
            if index >= 4:
                send.wait_send()
            dense_out[half, slot] = put_together(index, 2 + half).astype(jnp.bfloat16)
            send.start()
            if index >= len(units) - 4:
                at_end.append((None, [send]))

    def hand_on(index, plane_here, up):
        part, plane = units[index]
        unit = unit_of(part, plane)
        goal = plane_here + 1 if up else plane_here - 1
        slot = unit if up or goal != plane else CUTS * LINE + part
        send = push(
            sums.at[unit], passed.at[slot], pass_send.at[unit], pass_recv.at[slot], goal, e
        )
        send.start()
        return send

    def second(index):
        part, plane = units[index]
        unit = unit_of(part, plane)
        for half in range(2):
            wait_for(dense_in.at[half, unit], dense_recv.at[half, unit])
            whole = put_together(index, half) + dense_in[half, unit].astype(jnp.float32)
            sums[unit, :, half * CUT : (half + 1) * CUT] = whole.astype(jnp.bfloat16)
        if plane > 0:

            @pl.when(z == 0)
            def _():
                hand_on(index, 0, True)

        if plane < LINE - 1:

            @pl.when(z == LINE - 1)
            def _():
                hand_on(index, LINE - 1, False)

    def third(index, hop):
        part, plane = units[index]
        unit = unit_of(part, plane)
        ways = []
        if hop < plane and hop < LINE - 1:
            ways.append((hop, True))
        if LINE - 1 - hop > plane and LINE - 1 - hop > 0:
            ways.append((LINE - 1 - hop, False))
        for plane_here, up in ways:

            @pl.when(z == plane_here)
            def _():
                wait_for(passed.at[unit], pass_recv.at[unit])
                total = sums[unit].astype(jnp.float32) + passed[unit].astype(jnp.float32)
                sums[unit] = total.astype(jnp.bfloat16)
                hand_on(index, plane_here, up)

    own = pl.ds(e, 1)
    gates_plane[:, own] = gate_grad_ref[:, own]
    gate_moves = in_plane_of(here, gate_grad_ref, gates_plane, gate_plane_send, gate_plane_recv)
    gate_moves_on = along_line(here, gates_plane, gate_out_ref, gate_line_send, gate_line_recv)
    for move in gate_moves:
        move.start()

    count = len(units)
    for ahead in range(AHEAD):
        compact(ahead)
    for step in range(count + 3):
        if step + AHEAD < count:
            compact(step + AHEAD)
        if step == 2:
            for owner in here.plane:
                wait_for(gates_plane.at[:, owner], gate_plane_recv.at[owner])
            gate_out_ref[z] = gates_plane[z]
            for move in gate_moves_on:
                move.start()
        if step < count:
            first(step)
        if 0 <= step - 1 < count:
            second(step - 1)
        for hop in (1, 2):
            if 0 <= step - 1 - hop < count:
                third(step - 1 - hop, hop)

    for plane in here.line:
        wait_for(gate_out_ref.at[plane], gate_line_recv.at[plane])
    for move in gate_moves + gate_moves_on:
        move.wait_send()
    for part in range(CUTS):
        unit = part * LINE + z
        for half in range(2):
            out_ref[:, cut_columns(half, part)] = sums[
                unit, :, half * CUT : (half + 1) * CUT
            ].astype(jnp.float32)
        for going, slot in ((z > 0, unit), (z < LINE - 1, CUTS * LINE + part)):

            @pl.when(going)
            def _():
                wait_for(passed.at[slot], pass_recv.at[slot])
                for half in range(2):
                    columns = cut_columns(half, part)
                    out_ref[:, columns] = out_ref[:, columns] + passed[
                        slot, :, half * CUT : (half + 1) * CUT
                    ].astype(jnp.float32)

    for _, sends in at_end:
        for send in sends:
            send.wait_send()
    for part, plane in units:
        unit = unit_of(part, plane)

        @pl.when(z != plane)
        def _():
            push(
                sums.at[unit], passed.at[unit], pass_send.at[unit], pass_recv.at[unit], z, here.sib
            ).wait_send()


def combine(rows, positions, gate_grad, collective_id):
    capacity = rows.shape[1]
    bf16 = jnp.bfloat16
    dma = pltpu.SemaphoreType.DMA
    units = CUTS * LINE
    return pl.pallas_call(
        combine_kernel,
        out_shape=[
            jax.ShapeDtypeStruct((DEVICE_TOKENS, MODEL_WIDTH), jnp.float32),
            jax.ShapeDtypeStruct(GATE_SHAPE, jnp.float32),
        ],
        in_specs=[
            pl.BlockSpec(memory_space=pltpu.VMEM),
            pl.BlockSpec(memory_space=pltpu.VMEM),
            pl.BlockSpec(memory_space=pl.ANY),
        ],
        out_specs=[pl.BlockSpec(memory_space=pltpu.VMEM)] * 2,
        scratch_shapes=[
            pltpu.VMEM(GATE_SHAPE, jnp.float32),
            pltpu.VMEM((units, 4, 4 * capacity, CUT), bf16),
            pltpu.VMEM((2, 4, DEVICE_TOKENS, CUT), bf16),
            pltpu.VMEM((2, units, DEVICE_TOKENS, CUT), bf16),
            pltpu.VMEM((units, DEVICE_TOKENS, 2 * CUT), bf16),
            pltpu.VMEM((units + CUTS, DEVICE_TOKENS, 2 * CUT), bf16),
            dma((units, 12)),
            dma((units, 4, 4)),
            dma((2, 4)),
            dma((2, units)),
            dma((units,)),
            dma((units + CUTS,)),
            dma((PLANE,)),
            dma((PLANE,)),
            dma((LINE,)),
            dma((LINE,)),
        ],
        compiler_params=pltpu.CompilerParams(
            collective_id=collective_id, has_side_effects=True, vmem_limit_bytes=60 * 2**20
        ),
    )(positions, gate_grad, rows)


def near_first(z):
    power_of_four = (
        1 + 3 * z + lax.div(z * (z - 1), 2) * 9 + lax.div(z * (z - 1) * (z - 2), 6) * 27
    )
    orders = ((0, 1, 2, 3), (1, 0, 2, 3), (2, 3, 1, 0), (3, 2, 1, 0))
    tables = [
        sum(order[step] * 4**plane for plane, order in enumerate(orders)) for step in range(LINE)
    ]
    return [lax.rem(lax.div(jnp.int32(table), power_of_four), 4) for table in tables]


def wait_for(buffer, sem):
    pltpu.make_async_copy(buffer, buffer, sem).wait()


def spread_in_plane(here, whole, rows, halves, plane, recv, send, number, at_end, mine):
    z = here.z

    def piece(owner, half):
        start, size = halves[half]
        return whole.at[pl.ds((plane * PLANE + owner) * rows + start, size)]

    def to(owner, half, goal, count):
        copy = push(
            piece(owner, half),
            piece(owner, half),
            send.at[number, count],
            recv.at[plane * PLANE + owner, half],
            z,
            goal,
        )
        copy.start()
        at_end.append((None, [copy]))

    def arrived(owner, half):
        wait_for(piece(owner, half), recv.at[plane * PLANE + owner, half])

    ways = range(len(halves))

    def first():
        for half in ways:
            mine(half)
            to(here.e, half, here.x_same, 3 * half)
            to(here.e, half, here.y_same, 3 * half + 1)
            to(here.e, half, here.sib, 3 * half + 2)

    def second():
        for half in ways:
            arrived(here.x_same, half)
            if half == len(halves) - 1:
                to(here.x_same, half, here.y_same, 6)
            to(here.x_same, half, here.sib, 7 + half)
            arrived(here.y_same, half)
            if half == 0 and len(halves) > 1:
                to(here.y_same, half, here.x_same, 9)
            to(here.y_same, half, here.sib, 10 + half)

    def third():
        for half in ways:
            arrived(here.d_same, half)
            to(here.d_same, half, here.sib, 12 + half)

    def last():
        for owner in (here.sib, here.x_other, here.y_other, here.d_other):
            for half in ways:
                arrived(owner, half)

    return first, second, third, last


def finish(at_end):
    for go, sends in at_end:
        if go is None:
            for send in sends:
                send.wait_send()
        else:

            @pl.when(go)
            def _():
                for send in sends:
                    send.wait_send()


def halves_of(rows):
    return ((0, rows // 2), (rows // 2, rows // 2)) if rows >= 32 else ((0, rows),)


def gather_kernel(kinds, *refs):
    total = len(kinds)
    sources, wholes, scratch = refs[:total], refs[total : 2 * total], refs[2 * total :]
    here = Place()
    z, e = here.z, here.e
    here.greet()
    planes = near_first(z)
    at_end = []
    locals_ = []
    steps = [[] for _ in range(LINE)]
    arrays = []
    for index, (source, whole) in enumerate(zip(sources, wholes)):
        recv, send, line_send, own = scratch[4 * index : 4 * index + 4]
        passing = scratch[4 * total + index]
        kind = kinds[index]
        rows = source.shape[0] // (PLANE if kind == "weight" else 1)
        halves = halves_of(rows)
        arrays.append((kind, source, whole, rows, halves, recv, send, line_send))
        if kind == "block":
            base = (z * PLANE + e) * rows
        else:
            base = z * source.shape[0]
        first = pltpu.make_async_copy(source, passing, own.at[0])
        first.start()
        goal = whole.at[pl.ds(base, source.shape[0])]
        locals_.append((kind, first, pltpu.make_async_copy(passing, goal, own.at[1])))

    def line_piece(array, plane, half):
        kind, _, whole, rows, halves, _, _, _ = array
        start, size = halves[half]
        owner = plane if kind in ("plane", "late") else plane * PLANE + e
        return whole.at[pl.ds(owner * rows + start, size)]

    def line_sem(array, plane, half):
        owner = plane if array[0] in ("plane", "late") else plane * PLANE + e
        return array[5].at[owner, half]

    def along(array, step, half):
        plane = planes[step]
        kind, source, _, rows, halves, _, _, line_send = array
        for direction in range(2):
            if direction == 0:
                go = (plane <= z) & (z < LINE - 1)
                goal = z + 1
            else:
                go = (plane >= z) & (z > 0)
                goal = z - 1
            if step == 0:
                start, size = halves[half]
                offset = e * rows + start if kind == "weight" else start
                origin = source.at[pl.ds(offset, size)]
            else:
                origin = line_piece(array, plane, half)
            copy = push(
                origin,
                line_piece(array, plane, half),
                line_send.at[step, half, direction],
                line_sem(array, plane, half),
                goal,
                e,
            )

            @pl.when(go)
            def _():
                copy.start()

            at_end.append((go, [copy]))

    for array in arrays:
        if array[0] != "late":
            for half in range(len(array[4])):
                along(array, 0, half)
    for _, first, second in locals_:
        first.wait()
        second.start()
    for kind, _, second in locals_:
        if kind == "block":
            second.wait()

    later = []

    def arrive(step):
        work = []
        for array in arrays:
            kind, _, whole, rows, halves, recv, send, _ = array

            def mine(half, array=array):
                if step > 0:
                    wait_for(
                        line_piece(array, planes[step], half),
                        line_sem(array, planes[step], half),
                    )
                    along(array, step, half)

            if kind == "late":
                continue
            if kind == "plane" or (kind == "weight" and step == 0):
                if step > 0:
                    for half in range(len(halves)):
                        mine(half)
                continue
            first, second, third, last = spread_in_plane(
                here, whole, rows, halves, planes[step], recv, send, step, at_end, mine
            )
            first()
            work.append((second, third, last))
        later.append(work)

    def arrive_late(step):
        for array in arrays:
            if array[0] == "late":
                for half in range(len(array[4])):
                    if step > 0:
                        wait_for(
                            line_piece(array, planes[step], half),
                            line_sem(array, planes[step], half),
                        )
                    along(array, step, half)

    for step in range(LINE + 2):
        if step < LINE:
            arrive(step)
        if step >= 2:
            arrive_late(step - 2)
        if 0 <= step - 1 < LINE:
            for second, _, _ in later[step - 1]:
                second()
        if 0 <= step - 2 < LINE:
            for _, third, _ in later[step - 2]:
                third()
    for work in later:
        for _, _, last in work:
            last()
    for kind, _, second in locals_:
        if kind != "block":
            second.wait()
    finish(at_end)


def gather_all(weights, line, late, block, collective_id):
    sources = tuple(weights) + (line, late, block)
    kinds = ("weight",) * len(weights) + ("plane", "late", "block")
    parts = [LINE] * (len(sources) - 1) + [LINE * PLANE]
    dma = pltpu.SemaphoreType.DMA
    scratch = []
    for _ in sources:
        scratch += [dma((LINE * PLANE, 2)), dma((LINE, 16)), dma((LINE, 2, 2)), dma((2,))]
    scratch += [pltpu.VMEM(array.shape, array.dtype) for array in sources]
    return pl.pallas_call(
        functools.partial(gather_kernel, kinds),
        out_shape=[
            jax.ShapeDtypeStruct((array.shape[0] * part,) + array.shape[1:], array.dtype)
            for array, part in zip(sources, parts)
        ],
        in_specs=[pl.BlockSpec(memory_space=pl.ANY)] * len(sources),
        out_specs=[pl.BlockSpec(memory_space=pl.ANY)] * len(sources),
        scratch_shapes=scratch,
        compiler_params=pltpu.CompilerParams(
            collective_id=collective_id, has_side_effects=True, vmem_limit_bytes=32 * 2**20
        ),
    )(*sources)


def add_into(goal, *terms):
    rows, columns = goal.shape

    def some(index, carry):
        at = pl.ds(pl.multiple_of(index * 16, 16), 16)
        for start in range(0, columns, 1024):
            cut = slice(start, start + 1024)
            total = goal[at, cut].astype(jnp.float32)
            for term in terms:
                total = total + term[at, cut].astype(jnp.float32)
            goal[at, cut] = total.astype(goal.dtype)
        return carry

    lax.fori_loop(0, rows // 16, some, 0)


def reduce_kernel(count, *refs):
    sources, wholes, scratch = refs[:count], refs[count : 2 * count], refs[2 * count :]
    here = Place()
    z, e = here.z, here.e
    here.greet()
    at_end = []
    owners = (here.d_same, here.x_same, here.y_same, here.e)
    other_owners = (here.d_other, here.x_other, here.y_other, here.sib)
    units = [(plane, index) for index in range(count) for plane in FAR_FIRST]
    names = (
        "held", "sib", "half", "side", "passed",
        "held_recv", "sib_recv", "sib_send", "half_recv", "half_send",
        "side_recv", "side_send", "pass_recv", "pass_send", "own", "out_recv", "out_send",
    )
    per = len(names)
    buffers = [dict(zip(names, scratch[per * i : per * i + per])) for i in range(count)]
    rows_of = [source.shape[0] // (LINE * PLANE) for source in sources]

    def sent(copy):
        copy.start()
        at_end.append((None, [copy]))

    def load(number):
        plane, index = units[number]
        b, rows, source = buffers[index], rows_of[index], sources[index]
        for kind in range(4):
            mine = source.at[pl.ds((plane * PLANE + owners[kind]) * rows, rows)]
            theirs = source.at[pl.ds((plane * PLANE + other_owners[kind]) * rows, rows)]
            sent(
                push(
                    theirs,
                    b["sib"].at[plane, kind],
                    b["sib_send"].at[plane, kind],
                    b["sib_recv"].at[plane, kind],
                    z,
                    here.sib,
                )
            )
            pltpu.make_async_copy(
                mine, b["held"].at[plane, kind], b["held_recv"].at[plane, kind]
            ).start()

    def both(number, kind):
        plane, index = units[number]
        b = buffers[index]
        wait_for(b["held"].at[plane, kind], b["held_recv"].at[plane, kind])
        wait_for(b["sib"].at[plane, kind], b["sib_recv"].at[plane, kind])
        add_into(b["held"].at[plane, kind], b["sib"].at[plane, kind])

    def first(number):
        plane, index = units[number]
        b, rows = buffers[index], rows_of[index]
        both(number, 0)
        for half, goal in enumerate((here.y_same, here.x_same)):
            at = pl.ds(half * rows // 2, rows // 2)
            sent(
                push(
                    b["held"].at[plane, 0, at],
                    b["half"].at[plane, at],
                    b["half_send"].at[plane, half],
                    b["half_recv"].at[plane, half],
                    z,
                    goal,
                )
            )
        both(number, 1)
        both(number, 2)

    def second(number):
        plane, index = units[number]
        b, rows = buffers[index], rows_of[index]
        for half, goal in enumerate((here.x_same, here.y_same)):
            at = pl.ds(half * rows // 2, rows // 2)
            wait_for(b["half"].at[plane, at], b["half_recv"].at[plane, half])
            add_into(b["held"].at[plane, 1 + half, at], b["half"].at[plane, at])
            sent(
                push(
                    b["held"].at[plane, 1 + half],
                    b["side"].at[half, plane],
                    b["side_send"].at[half, plane],
                    b["side_recv"].at[half, plane],
                    z,
                    goal,
                )
            )
        both(number, 3)

    def hand_on(number, plane_here, up):
        plane, index = units[number]
        b = buffers[index]
        goal = plane_here + 1 if up else plane_here - 1
        slot = plane if up or goal != plane else LINE
        push(
            b["held"].at[plane, 3],
            b["passed"].at[slot],
            b["pass_send"].at[plane],
            b["pass_recv"].at[slot],
            goal,
            e,
        ).start()

    def third(number):
        plane, index = units[number]
        b = buffers[index]
        for half in range(2):
            wait_for(b["side"].at[half, plane], b["side_recv"].at[half, plane])
        add_into(b["held"].at[plane, 3], b["side"].at[0, plane], b["side"].at[1, plane])
        if plane > 0:

            @pl.when(z == 0)
            def _():
                hand_on(number, 0, True)

        if plane < LINE - 1:

            @pl.when(z == LINE - 1)
            def _():
                hand_on(number, LINE - 1, False)

    def hop(number, distance):
        plane, index = units[number]
        b = buffers[index]
        ways = []
        if distance < plane and distance < LINE - 1:
            ways.append((distance, True))
        if LINE - 1 - distance > plane and LINE - 1 - distance > 0:
            ways.append((LINE - 1 - distance, False))
        for plane_here, up in ways:

            @pl.when(z == plane_here)
            def _():
                wait_for(b["passed"].at[plane], b["pass_recv"].at[plane])
                add_into(b["held"].at[plane, 3], b["passed"].at[plane])
                hand_on(number, plane_here, up)

    def spread(index):
        b, rows, whole = buffers[index], rows_of[index], wholes[index]
        for going, slot in ((z > 0, z), (z < LINE - 1, LINE)):

            @pl.when(going)
            def _():
                wait_for(b["passed"].at[slot], b["pass_recv"].at[slot])
                add_into(b["held"].at[z, 3], b["passed"].at[slot])

        copy = pltpu.make_async_copy(
            b["held"].at[z, 3], whole.at[pl.ds(e * rows, rows)], b["own"].at[0]
        )
        copy.start()
        copy.wait()
        return spread_in_plane(
            here,
            whole,
            rows,
            halves_of(rows),
            0,
            b["out_recv"],
            b["out_send"],
            0,
            at_end,
            lambda half: None,
        )

    steps = len(units)
    ready = LINE - 1 + 2 + 3
    spreads = {}
    load(0)
    load(1)
    for step in range((count - 1) * LINE + ready + 3):
        if step + 2 < steps:
            load(step + 2)
        if step < steps:
            first(step)
        if 0 <= step - 1 < steps:
            second(step - 1)
        if 0 <= step - 2 < steps:
            third(step - 2)
        for distance in (1, 2):
            if 0 <= step - 2 - distance < steps:
                hop(step - 2 - distance, distance)
        for index in range(count):
            stage = step - index * LINE - ready
            if stage == 0:
                spreads[index] = spread(index)
            if 0 <= stage < 3:
                spreads[index][stage]()
    for index in range(count):
        spreads[index][3]()
    finish(at_end)
    for plane, index in units:
        b = buffers[index]

        @pl.when(z != plane)
        def _():
            push(
                b["held"].at[plane, 3],
                b["passed"].at[plane],
                b["pass_send"].at[plane],
                b["pass_recv"].at[plane],
                z,
                here.sib,
            ).wait_send()


def reduce_all(arrays, collective_id):
    dma = pltpu.SemaphoreType.DMA
    scratch = []
    for array in arrays:
        rows = array.shape[0] // (LINE * PLANE)
        block = (rows, array.shape[1])
        scratch += [
            pltpu.VMEM((LINE, 4) + block, array.dtype),
            pltpu.VMEM((LINE, 4) + block, array.dtype),
            pltpu.VMEM((LINE,) + block, array.dtype),
            pltpu.VMEM((2, LINE) + block, array.dtype),
            pltpu.VMEM((LINE + 1,) + block, array.dtype),
            dma((LINE, 4)),
            dma((LINE, 4)),
            dma((LINE, 4)),
            dma((LINE, 2)),
            dma((LINE, 2)),
            dma((2, LINE)),
            dma((2, LINE)),
            dma((LINE + 1,)),
            dma((LINE,)),
            dma((1,)),
            dma((PLANE, 2)),
            dma((1, 16)),
        ]
    return pl.pallas_call(
        functools.partial(reduce_kernel, len(arrays)),
        out_shape=[
            jax.ShapeDtypeStruct((array.shape[0] // LINE, array.shape[1]), array.dtype)
            for array in arrays
        ],
        in_specs=[pl.BlockSpec(memory_space=pl.ANY)] * len(arrays),
        out_specs=[pl.BlockSpec(memory_space=pl.ANY)] * len(arrays),
        scratch_shapes=scratch,
        compiler_params=pltpu.CompilerParams(
            collective_id=collective_id, has_side_effects=True, vmem_limit_bytes=60 * 2**20
        ),
    )(*arrays)


ROWS = 256
FORWARD_ROWS = 256
LOG2_E = 1.4426950408889634
GROUP = QUERY_HEADS // KEY_VALUE_HEADS
SCORE_SCALE = HEAD_SIZE ** (-0.5)


def across(left, right, contract):
    return lax.dot_general(
        left, right, ((contract[:1], contract[1:]), ((), ())), preferred_element_type=jnp.float32
    )


def head_norm(raw, gain):
    scale = lax.rsqrt(jnp.mean(raw * raw, axis=-1, keepdims=True) + EPSILON)
    unit = raw * scale
    return scale, unit, unit * gain


def turned(rows, sine):
    return pltpu.roll(rows, HEAD_SIZE // 2, 1) * sine


def masked(segment_column, segment_row):
    shape = (segment_column.shape[0], segment_row.shape[1])
    before = lax.broadcasted_iota(jnp.int32, shape, 1) <= lax.broadcasted_iota(jnp.int32, shape, 0)
    return jnp.where(before & (segment_column == segment_row), 0.0, -1e30)


def row_blocks(length, rows=ROWS):
    return [(start, start + rows) for start in range(0, length, rows)]


def attention_kernel(
    query_ref,
    key_ref,
    value_ref,
    cosine_ref,
    sine_ref,
    query_gain_ref,
    key_gain_ref,
    column_ref,
    row_ref,
    mixed_ref,
    query_rot_ref,
    key_rot_ref,
    value_low_ref,
    total_ref,
    bias,
):
    low = jnp.bfloat16
    length = bias.shape[0]

    @pl.when(pl.program_id(0) == 0)
    def _():
        bias[...] = masked(column_ref[...], row_ref[...])

    cosine, sine = cosine_ref[...], sine_ref[...]
    _, _, key = head_norm(key_ref[...], key_gain_ref[...])
    key_rot = (key * cosine + turned(key, sine)).astype(low)
    key_rot_ref[...] = key_rot
    value = value_ref[...].astype(low)
    value_low_ref[...] = value
    totals = []
    for head in range(GROUP):
        columns = slice(head * HEAD_SIZE, (head + 1) * HEAD_SIZE)
        _, _, query = head_norm(query_ref[:, columns], query_gain_ref[...])
        query_rot = (query * cosine + turned(query, sine)).astype(low)
        query_rot_ref[:, columns] = query_rot
        parts = []
        for start, end in row_blocks(length, FORWARD_ROWS):
            scores = across(query_rot[start:end], key_rot[:end], (1, 1)) + bias[start:end, :end]
            peak = jnp.max(scores, axis=-1, keepdims=True)
            weights = jnp.exp2((scores - peak) * (SCORE_SCALE * LOG2_E))
            total = jnp.sum(weights, axis=-1, keepdims=True)
            mixed = across(weights.astype(low), value[:end], (1, 0)) * (1.0 / total)
            mixed_ref[start:end, columns] = mixed.astype(low)
            parts.append(peak * SCORE_SCALE + jnp.log(total))
        totals.append(jnp.concatenate(parts, axis=0))
    total_ref[0] = jnp.concatenate(totals, axis=1)


def attention(qkv, segments, cosine, sine, query_gain, key_gain):
    length = qkv.shape[0]
    width = GROUP * HEAD_SIZE
    low = jnp.bfloat16
    whole = lambda *shape: pl.BlockSpec(shape, lambda j: (0,) * len(shape))
    heads = lambda first: pl.BlockSpec((length, HEAD_SIZE), lambda j: (0, first + j))
    key_start = QUERY_HEADS
    return pl.pallas_call(
        attention_kernel,
        grid=(KEY_VALUE_HEADS,),
        in_specs=[
            pl.BlockSpec((length, width), lambda j: (0, j)),
            heads(key_start),
            heads(key_start + KEY_VALUE_HEADS),
            whole(length, HEAD_SIZE),
            whole(length, HEAD_SIZE),
            whole(1, HEAD_SIZE),
            whole(1, HEAD_SIZE),
            whole(length, 1),
            whole(1, length),
        ],
        out_specs=[
            pl.BlockSpec((length, width), lambda j: (0, j)),
            pl.BlockSpec((length, width), lambda j: (0, j)),
            heads(0),
            heads(0),
            pl.BlockSpec((1, length, GROUP), lambda j: (j, 0, 0)),
        ],
        out_shape=[
            jax.ShapeDtypeStruct((length, QUERY_HEADS * HEAD_SIZE), low),
            jax.ShapeDtypeStruct((length, QUERY_HEADS * HEAD_SIZE), low),
            jax.ShapeDtypeStruct((length, KEY_VALUE_HEADS * HEAD_SIZE), low),
            jax.ShapeDtypeStruct((length, KEY_VALUE_HEADS * HEAD_SIZE), low),
            jax.ShapeDtypeStruct((KEY_VALUE_HEADS, length, GROUP), jnp.float32),
        ],
        scratch_shapes=[pltpu.VMEM((length, length), jnp.float32)],
        compiler_params=pltpu.CompilerParams(vmem_limit_bytes=48 * 2**20),
    )(qkv, qkv, qkv, cosine, sine, query_gain, key_gain, segments.T, segments)


def attention_back_kernel(
    query_ref,
    key_ref,
    query_rot_ref,
    key_rot_ref,
    value_ref,
    mixed_grad_ref,
    total_ref,
    cosine_ref,
    sine_ref,
    query_gain_ref,
    key_gain_ref,
    column_ref,
    row_ref,
    query_out_ref,
    key_out_ref,
    value_out_ref,
    gains_ref,
    bias,
):
    low = jnp.bfloat16
    length = bias.shape[0]

    @pl.when(pl.program_id(0) == 0)
    def _():
        bias[...] = masked(column_ref[...], row_ref[...])
        gains_ref[...] = jnp.zeros_like(gains_ref)

    cosine, sine = cosine_ref[...], sine_ref[...]
    key_rot, value = key_rot_ref[...], value_ref[...]

    def before_norm(grad_rot, raw, gain):
        grad = grad_rot * cosine - turned(grad_rot, sine)
        scale, unit, _ = head_norm(raw, gain)
        gain_grad = jnp.sum(grad * unit, axis=0, keepdims=True)
        pulled = grad * gain
        back = scale * (pulled - unit * jnp.mean(pulled * unit, axis=-1, keepdims=True))
        return back.astype(low), gain_grad

    blocks = row_blocks(length)
    key_grads = [jnp.zeros((ROWS, HEAD_SIZE), jnp.float32) for _ in blocks]
    value_grads = [jnp.zeros((ROWS, HEAD_SIZE), jnp.float32) for _ in blocks]
    query_gain_grad = jnp.zeros((1, HEAD_SIZE), jnp.float32)
    for head in range(GROUP):
        columns = slice(head * HEAD_SIZE, (head + 1) * HEAD_SIZE)
        query_rot = query_rot_ref[:, columns]
        mixed_grad = mixed_grad_ref[:, columns]
        total = total_ref[0, :, head : head + 1]
        parts = []
        for start, end in blocks:
            scores = across(query_rot[start:end], key_rot[:end], (1, 1)) * SCORE_SCALE
            probs = jnp.exp(scores + bias[start:end, :end] - total[start:end])
            prob_grad = across(mixed_grad[start:end], value[:end], (1, 1))
            weighted = prob_grad * probs
            row_sum = jnp.sum(weighted, axis=-1, keepdims=True)
            score_low = (weighted - probs * row_sum).astype(low)
            probs_low = probs.astype(low)
            parts.append(across(score_low, key_rot[:end], (1, 0)) * SCORE_SCALE)
            key_part = across(score_low, query_rot[start:end], (0, 0))
            value_part = across(probs_low, mixed_grad[start:end], (0, 0))
            for index, (first, last) in enumerate(blocks):
                if last <= end:
                    key_grads[index] = key_grads[index] + key_part[first:last]
                    value_grads[index] = value_grads[index] + value_part[first:last]
        back, gain_grad = before_norm(
            jnp.concatenate(parts, axis=0), query_ref[:, columns], query_gain_ref[...]
        )
        query_out_ref[:, columns] = back
        query_gain_grad = query_gain_grad + gain_grad
    back, key_gain_grad = before_norm(
        jnp.concatenate(key_grads, axis=0) * SCORE_SCALE, key_ref[...], key_gain_ref[...]
    )
    key_out_ref[...] = back
    value_out_ref[...] = jnp.concatenate(value_grads, axis=0).astype(low)
    gains_ref[0:1] += query_gain_grad
    gains_ref[1:2] += key_gain_grad


def attention_back(
    qkv, query_rot, key_rot, value, mixed_grad, totals, segments, cosine, sine, query_gain, key_gain
):
    length = qkv.shape[0]
    width = GROUP * HEAD_SIZE
    low = jnp.bfloat16
    whole = lambda *shape: pl.BlockSpec(shape, lambda j: (0,) * len(shape))
    heads = lambda first: pl.BlockSpec((length, HEAD_SIZE), lambda j: (0, first + j))
    wide = pl.BlockSpec((length, width), lambda j: (0, j))
    return pl.pallas_call(
        attention_back_kernel,
        grid=(KEY_VALUE_HEADS,),
        in_specs=[
            wide,
            heads(QUERY_HEADS),
            wide,
            heads(0),
            heads(0),
            wide,
            pl.BlockSpec((1, length, GROUP), lambda j: (j, 0, 0)),
            whole(length, HEAD_SIZE),
            whole(length, HEAD_SIZE),
            whole(1, HEAD_SIZE),
            whole(1, HEAD_SIZE),
            whole(length, 1),
            whole(1, length),
        ],
        out_specs=[wide, heads(0), heads(0), whole(8, HEAD_SIZE)],
        out_shape=[
            jax.ShapeDtypeStruct((length, QUERY_HEADS * HEAD_SIZE), low),
            jax.ShapeDtypeStruct((length, KEY_VALUE_HEADS * HEAD_SIZE), low),
            jax.ShapeDtypeStruct((length, KEY_VALUE_HEADS * HEAD_SIZE), low),
            jax.ShapeDtypeStruct((8, HEAD_SIZE), jnp.float32),
        ],
        scratch_shapes=[pltpu.VMEM((length, length), jnp.float32)],
        compiler_params=pltpu.CompilerParams(vmem_limit_bytes=56 * 2**20),
    )(
        qkv,
        qkv,
        query_rot,
        key_rot,
        value,
        mixed_grad,
        totals,
        cosine,
        sine,
        query_gain,
        key_gain,
        segments.T,
        segments,
    )


UNITS = 16
GATE_SHAPE = (LINE, PLANE, 1, DEVICE_TOKENS)
LAG = 4
CHUNK = 2


def expert_kernel(
    pos_ref,
    gates_ref,
    w_gate_ref,
    w_up_ref,
    w_down_ref,
    routed_ref,
    cotangent_ref,
    early_line_ref,
    early_x_ref,
    early_y_ref,
    routed_rows_ref,
    cotangent_rows_ref,
    out_ref,
    out_second_ref,
    back_ref,
    act_ref,
    gate_low_ref,
    up_low_ref,
    gate_grad_ref,
    line,
    dense,
    own_held,
    near,
    side,
    gates_line,
    gates_here,
    picked,
    taken,
    out_held,
    back_held,
    act_held,
    gate_held,
    up_held,
    line_send,
    line_recv,
    dense_send,
    dense_recv,
    side_send,
    row_send,
    row_recv,
    own_sem,
    near_sem,
    side_sem,
    taken_sem,
    put_sem,
    gate_line_send,
    gate_line_recv,
    gate_plane_send,
    gate_plane_recv,
):
    here = Place()
    z, e = here.z, here.e
    capacity = out_ref.shape[1]
    low, f32 = jnp.bfloat16, jnp.float32
    rows_refs = (routed_rows_ref, cotangent_rows_ref)
    here.greet()
    targets = target_sets(here)
    planes = near_first(z)
    packed = planes[0] + 4 * planes[1] + 16 * planes[2] + 64 * planes[3]
    inputs = (routed_ref, cotangent_ref)

    def plane_of(step):
        power = (
            1
            + 3 * step
            + lax.div(step * (step - 1), 2) * 9
            + lax.div(step * (step - 1) * (step - 2), 6) * 27
        )
        return lax.rem(lax.div(packed, power), 4)

    def unit(i):
        return plane_of(lax.div(i, 4)), lax.rem(lax.div(i, 2), 2), lax.rem(i, 2)

    def columns(half, part):
        return pl.ds(pl.multiple_of(half * 2 * PART + part * PART, PART), PART)

    firsts = [
        pltpu.make_async_copy(inputs[stream], own_held.at[stream], near_sem.at[stream])
        for stream in range(2)
    ]
    for first in firsts:
        first.start()
    for stream in range(2):
        firsts[stream].wait()
        for part in range(stream, 2):
            for half in range(2):
                pltpu.make_async_copy(
                    own_held.at[stream, :, part_columns(half, part)],
                    line.at[stream, part, z, half],
                    line_recv.at[stream, part, z, half],
                ).start()
    at_an_end = (z == 0) | (z == LINE - 1)
    gates_line[z] = gates_ref[z]
    gate_moves = along_line(here, gates_ref, gates_line, gate_line_send, gate_line_recv)
    gate_moves_on = in_plane_of(here, gates_line, gates_here, gate_plane_send, gate_plane_recv)
    for move in gate_moves:
        move.start()

    def spread_gates():
        for plane in here.line:
            wait_for(gates_line.at[plane], gate_line_recv.at[plane])
        own = pl.ds(e, 1)
        gates_here[:, own] = gates_line[:, own]
        for move in gate_moves_on:
            move.start()

    def wait_gates():
        for owner in here.plane:
            wait_for(gates_here.at[:, owner], gate_plane_recv.at[owner])

    def forwards(i):
        plane, stream, part = unit(i)
        out = []
        for half in range(2):
            for direction in range(2):
                goal = z + 1 - 2 * direction
                out.append(
                    push(
                        line.at[stream, part, plane, half],
                        line.at[stream, part, plane, half],
                        line_send.at[i, half, direction],
                        line_recv.at[stream, part, plane, half],
                        goal,
                        e,
                    )
                )
        return out

    def side_forwards(i):
        plane, stream, part = unit(i)
        return [
            push(
                dense.at[stream, part, plane, half],
                dense.at[stream, part, plane, half],
                side_send.at[lax.div(i, 4), half, direction],
                dense_recv.at[stream, part, plane, half],
                z + 1 - 2 * direction,
                e,
            )
            for half in range(2)
            for direction in range(2)
        ]

    def along(i, sends, act):
        plane = unit(i)[0]

        @pl.when((plane <= z) & (z < LINE - 1))
        def _():
            act(sends[0])
            act(sends[2])

        @pl.when((plane >= z) & (z > 0))
        def _():
            act(sends[1])
            act(sends[3])

    def side_first(i):
        return lax.rem(i, 4) == 3

    def early(i):
        return lax.rem(i, 4) == 2

    def denses(i):
        plane, stream, part = unit(i)
        return [
            push(
                line.at[stream, part, plane, half],
                dense.at[stream, part, plane, half],
                dense_send.at[i, half],
                dense_recv.at[stream, part, plane, half],
                z,
                (here.x_same, here.y_same)[half],
            )
            for half in range(2)
        ]

    def pass_on(i):
        plane, stream, part = unit(i)
        for half in range(2):
            wait_for(line.at[stream, part, plane, half], line_recv.at[stream, part, plane, half])
        along(i, forwards(i), lambda send: send.start())

    def pass_side_on(i):
        plane, stream, part = unit(i)
        for half in range(2):
            wait_for(dense.at[stream, part, plane, half], dense_recv.at[stream, part, plane, half])
        along(i, side_forwards(i), lambda send: send.start())

    def arrive(i):
        plane, stream, part = unit(i)

        @pl.when(early(i))
        def _():
            for half in range(2):
                pltpu.make_async_copy(
                    early_line_ref.at[plane, :, pl.ds(half * PART, PART)],
                    near.at[half],
                    near_sem.at[half],
                ).start()

        @pl.when(jnp.logical_not(early(i)))
        def _():
            @pl.when((i >= 4) & at_an_end)
            def _():
                for half in range(2):
                    wait_for(
                        line.at[stream, part, plane, half], line_recv.at[stream, part, plane, half]
                    )

            for half in range(2):
                pltpu.make_async_copy(
                    line.at[stream, part, plane, half], near.at[half], near_sem.at[half]
                ).start()

            @pl.when(jnp.logical_not(side_first(i)))
            def _():
                for send in denses(i):
                    send.start()

    def arrive_side(i):
        plane, stream, part = unit(i)

        @pl.when(early(i))
        def _():
            for half, source in enumerate((early_x_ref, early_y_ref)):
                pltpu.make_async_copy(source.at[plane], side.at[half], side_sem.at[half]).start()

        @pl.when(jnp.logical_not(early(i)))
        def _():
            @pl.when(jnp.logical_not(side_first(i)) | ((i > 3) & at_an_end))
            def _():
                for half in range(2):
                    wait_for(
                        dense.at[stream, part, plane, half],
                        dense_recv.at[stream, part, plane, half],
                    )

            for half in range(2):
                pltpu.make_async_copy(
                    dense.at[stream, part, plane, half], side.at[half], side_sem.at[half]
                ).start()

    def picks(i, number, rows_ref=routed_rows_ref):
        plane, stream, part = unit(i)
        owner, half, experts = targets[number]
        block = plane * PLANE + owner
        slot = lax.rem(i, 2)
        goal = rows_ref.at[block, :, columns(half, part)]
        sem = row_recv.at[stream, block, half, part]
        out = []
        for k in range(4):
            rows = picked.at[slot, number, pl.ds(k * capacity, capacity)]
            if k == 0:
                out.append(pltpu.make_async_copy(rows, goal, own_sem.at[slot, number]))
            else:
                out.append(push(rows, goal, row_send.at[slot, number, k], sem, z, experts[k]))
        return block, slot, experts, out

    def pick(i, number, source):
        block, slot, experts, sends = picks(i, number)

        @pl.when(i >= 2)
        def _():
            for send in sends[1:]:
                send.wait_send()

        select = one_hot(pos_ref, experts, block, capacity)
        picked[slot, number] = jnp.dot(select, source[...], preferred_element_type=f32).astype(low)
        for stream in range(2):

            @pl.when(unit(i)[1] == stream)
            def _():
                for send in picks(i, number, rows_refs[stream])[3]:
                    send.start()

    def wait_own(i, number):
        picks(i, number)[3][0].wait()

    def pair(c):
        plane = plane_of(lax.div(c, 4))
        j = lax.rem(c, 4)
        owner = (
            e + lax.rem(j, 2) * (here.x_same - e) + lax.div(j, 2) * (here.y_same - e)
        )
        first = plane * PLANE + owner
        at = owner * LINE + plane
        owners = (owner, owner + here.sib - e)
        return j, first, first + here.sib - e, (at, at + (here.sib - e) * LINE, plane, owners)

    def takes(c):
        _, first, second, _ = pair(c)
        slot = lax.rem(c, 2)
        return [
            pltpu.make_async_copy(
                rows_refs[stream].at[block],
                taken.at[slot, stream, pl.ds(number * capacity, capacity)],
                taken_sem.at[slot, stream, number],
            )
            for stream in range(2)
            for number, block in enumerate((first, second))
        ]

    def take(c):
        j, first, second, _ = pair(c)

        def wait_rows(block, half):
            for stream in range(2):
                for part in range(2):
                    wait_for(
                        rows_refs[stream].at[block, :, part_columns(half, part)],
                        row_recv.at[stream, block, half, part],
                    )

        for half in range(2):
            wait_rows(second, half)

        @pl.when((j == 2) | (j == 3))
        def _():
            wait_rows(first, 0)

        @pl.when((j == 1) | (j == 3))
        def _():
            wait_rows(first, 1)

        for copy in takes(c):
            copy.start()

    def puts(c):
        _, first, second, out_at = pair(c)
        out = []
        for number, block in enumerate((first, second)):
            at = pl.ds(number * capacity, capacity)
            for kind, (held, goal) in enumerate(
                (
                    (out_held.at[:, pl.ds(0, MODEL_WIDTH // 2)], out_ref),
                    (out_held.at[:, pl.ds(MODEL_WIDTH // 2, MODEL_WIDTH // 2)], out_second_ref),
                    (back_held, back_ref),
                    (act_held, act_ref),
                    (gate_held, gate_low_ref),
                    (up_held, up_low_ref),
                )
            ):
                to = out_at[number] if kind < 2 else block
                out.append(
                    pltpu.make_async_copy(held.at[at], goal.at[to], put_sem.at[kind, number])
                )
        return out

    def compute(c):
        for copy in takes(c):
            copy.wait()

        @pl.when(c > 0)
        def _():
            for copy in puts(c - 1):
                copy.wait()

        slot = lax.rem(c, 2)
        _, first, second, (_, _, plane, owners) = pair(c)
        slots = lax.broadcasted_iota(jnp.int32, (capacity, DEVICE_TOKENS), 0)
        chosen = [slots == pos_ref[e, pl.ds(block, 1), :] for block in (first, second)]
        gates = jnp.concatenate(
            [
                jnp.sum(
                    jnp.where(mask, gates_here[plane, owner], 0.0), axis=1, keepdims=True
                )
                for mask, owner in zip(chosen, owners)
            ],
            axis=0,
        )
        rows = taken[slot, 0]
        gate_part = jnp.dot(rows, w_gate_ref[...], preferred_element_type=f32)
        up_part = jnp.dot(rows, w_up_ref[...], preferred_element_type=f32)
        sigmoid = 1.0 / (1.0 + jnp.exp(-gate_part))
        silu = gate_part * sigmoid
        act_low = (silu * up_part).astype(low)
        pull = across(taken[slot, 1], w_down_ref[...], (1, 1))
        act = act_low.astype(f32)
        row_grad = jnp.sum(act * pull, axis=1, keepdims=True)
        for number, owner in enumerate(owners):
            mine = row_grad[number * capacity : (number + 1) * capacity]
            gate_grad_ref[plane, owner] = jnp.sum(
                jnp.where(chosen[number], mine, 0.0), axis=0, keepdims=True
            )
        act_held[...] = (act * gates).astype(low)
        pull = pull * gates
        gate_low = (pull * up_part * (sigmoid * (1.0 + gate_part * (1.0 - sigmoid)))).astype(low)
        up_low = (pull * silu).astype(low)
        gate_held[...] = gate_low
        up_held[...] = up_low
        out_held[...] = (
            jnp.dot(act_low, w_down_ref[...], preferred_element_type=f32) * gates
        ).astype(low)
        back_held[...] = (
            across(gate_low, w_gate_ref[...], (1, 1)) + across(up_low, w_up_ref[...], (1, 1))
        ).astype(low)
        for copy in puts(c):
            copy.start()

    def step(i, carry):
        @pl.when((i > 0) & (i <= UNITS))
        def _():
            wait_own(i - 1, 0)
            wait_own(i - 1, 1)

        @pl.when(i < UNITS)
        def _():
            for half in range(2):
                wait_for(near.at[half], near_sem.at[half])
                pick(i, half, near.at[half])

        @pl.when((i > 0) & (i <= UNITS))
        def _():
            for half in range(2):
                wait_for(side.at[half], side_sem.at[half])
                pick(i - 1, 2 + half, side.at[half])

        @pl.when(i < UNITS - 1)
        def _():
            arrive(i + 1)

        @pl.when(i < UNITS)
        def _():
            arrive_side(i)

        @pl.when(i == 1)
        def _():
            spread_gates()

        @pl.when(i == LAG)
        def _():
            wait_gates()

        @pl.when(i >= LAG)
        def _():
            @pl.when(lax.rem(i - LAG, 4) == 0)
            def _():
                take(i - LAG)

            compute(i - LAG)

        @pl.when((i > 0) & (i <= UNITS))
        def _():
            wait_own(i - 1, 2)
            wait_own(i - 1, 3)

        @pl.when((i >= LAG) & (lax.rem(i - LAG, 4) != 3))
        def _():
            take(i - (LAG - 1))

        for first_step, last_step, ahead in ((1, 4, 3), (2, 5, 6), (5, 8, 7)):

            @pl.when(
                (i >= first_step)
                & (i <= last_step)
                & jnp.logical_not(at_an_end)
                & jnp.logical_not(early(i + ahead))
            )
            def _():
                pass_on(i + ahead)

        @pl.when(i == 1)
        def _():
            pass_side_on(i + 2)

        for at_step, ahead in ((5, 2), (6, 5), (10, 5)):

            @pl.when((i == at_step) & jnp.logical_not(at_an_end))
            def _():
                pass_side_on(i + ahead)

        return carry

    for i in (0, 1, 3):
        pass_on(jnp.int32(i))
    for send in denses(jnp.int32(3)):
        send.start()
    arrive(jnp.int32(0))
    lax.fori_loop(0, UNITS + LAG, step, 0)
    for copy in puts(UNITS - 1):
        copy.wait()
    for move in gate_moves + gate_moves_on:
        move.wait_send()
    for i in (UNITS - 2, UNITS - 1):
        for number in range(4):
            for send in picks(jnp.int32(i), number)[3][1:]:
                send.wait_send()

    def drain(i, carry):
        @pl.when(jnp.logical_not(early(i)))
        def _():
            along(i, forwards(i), lambda send: send.wait_send())

            @pl.when(jnp.logical_not(side_first(i)) | (i == 3))
            def _():
                for send in denses(i):
                    send.wait_send()

        @pl.when(side_first(i))
        def _():
            along(i, side_forwards(i), lambda send: send.wait_send())

        return carry

    lax.fori_loop(0, UNITS, drain, 0)


def dispatch_and_expert(
    routed,
    cotangent,
    early_line,
    early_sides,
    positions,
    gates,
    w_gate,
    w_up,
    w_down,
    capacity,
    collective_id,
):
    low, f32 = jnp.bfloat16, jnp.float32
    blocks = LINE * PLANE
    dma = pltpu.SemaphoreType.DMA
    wide = jax.ShapeDtypeStruct((blocks, capacity, MODEL_WIDTH), low)
    half_wide = jax.ShapeDtypeStruct((blocks, capacity, MODEL_WIDTH // 2), low)
    narrow = jax.ShapeDtypeStruct((blocks, capacity, w_gate.shape[1]), low)
    landing = jax.ShapeDtypeStruct((2, 2, LINE, 2, DEVICE_TOKENS, PART), low)
    vmem = pl.BlockSpec(memory_space=pltpu.VMEM)
    anywhere = pl.BlockSpec(memory_space=pl.ANY)
    chunk = CHUNK * capacity
    return pl.pallas_call(
        expert_kernel,
        out_shape=[
            wide,
            wide,
            half_wide,
            half_wide,
            wide,
            narrow,
            narrow,
            narrow,
            jax.ShapeDtypeStruct(GATE_SHAPE, f32),
            landing,
            landing,
        ],
        in_specs=[vmem] * 5 + [anywhere] * 5,
        out_specs=[anywhere] * 8 + [vmem] + [anywhere] * 2,
        scratch_shapes=[
            pltpu.VMEM((2, DEVICE_TOKENS, MODEL_WIDTH), low),
            pltpu.VMEM((2, DEVICE_TOKENS, PART), low),
            pltpu.VMEM((2, DEVICE_TOKENS, PART), low),
            pltpu.VMEM(GATE_SHAPE, f32),
            pltpu.VMEM(GATE_SHAPE, f32),
            pltpu.VMEM((2, 4, 4 * capacity, PART), low),
            pltpu.VMEM((2, 2, chunk, MODEL_WIDTH), low),
            pltpu.VMEM((chunk, MODEL_WIDTH), low),
            pltpu.VMEM((chunk, MODEL_WIDTH), low),
            pltpu.VMEM((chunk, w_gate.shape[1]), low),
            pltpu.VMEM((chunk, w_gate.shape[1]), low),
            pltpu.VMEM((chunk, w_gate.shape[1]), low),
            dma((UNITS, 2, 2)),
            dma((2, 2, LINE, 2)),
            dma((UNITS, 2)),
            dma((2, 2, LINE, 2)),
            dma((LINE, 2, 2)),
            dma((2, 4, 4)),
            dma((2, blocks, 2, 2)),
            dma((2, 4)),
            dma((2,)),
            dma((2,)),
            dma((2, 2, 2)),
            dma((6, 2)),
            dma((LINE,)),
            dma((LINE,)),
            dma((PLANE,)),
            dma((PLANE,)),
        ],
        compiler_params=pltpu.CompilerParams(
            collective_id=collective_id, has_side_effects=True, vmem_limit_bytes=60 * 2**20
        ),
    )(positions, gates, w_gate, w_up, w_down, routed, cotangent, early_line, *early_sides)[:9]


def on_device(
    tokens,
    segments,
    routes,
    w_query,
    key_projection,
    value_projection,
    w_out,
    w_router,
    gain_attn,
    gain_ffn,
    gain_query,
    key_head_gain,
    w_gate,
    w_up,
    w_down,
    cotangent,
):
    f32 = jnp.float32
    brain_float = jnp.bfloat16
    sequence_length = tokens.shape[0]
    planes = lax.axis_size("fsdp")
    experts = planes * lax.axis_size("expert")
    capacity = 5 * DEVICE_TOKENS * TOP // (4 * experts)
    expert_ids = jnp.arange(experts, dtype=jnp.int32)
    my_expert = lax.axis_index("fsdp") * lax.axis_size("expert") + lax.axis_index("expert")
    in_blocks = (planes, experts) == (LINE, LINE * PLANE)

    small = (w_router, gain_attn, gain_ffn, gain_query, key_head_gain)
    small_sizes = [array.size for array in small]
    local_qkv = jnp.concatenate([w_query, key_projection, value_projection], axis=1)
    small_flat = jnp.concatenate([array.reshape(-1) for array in small])
    if in_blocks:
        width = -(-small_flat.size // (16 * 128)) * 128
        small_flat = jnp.pad(small_flat, (0, 16 * width - small_flat.size))
        cot_front = jnp.concatenate(
            [cotangent[:, :PART], cotangent[:, 2 * PART : 3 * PART]], axis=1
        )
        full_qkv, full_out, small_all, cot_line, routes_all = gather_all(
            (local_qkv, w_out), small_flat.reshape(16, width), cot_front, routes.T, 3
        )
        cot_line = cot_line.reshape(planes, sequence_length, 2 * PART)
        cot_sides = [
            lax.ppermute(
                cot_line[:, :, half * PART : (half + 1) * PART],
                "expert",
                [(device, device ^ (2 << half)) for device in range(PLANE)],
            )
            for half in range(2)
        ]
        small_all = small_all.reshape(planes, -1)
        routes_all = routes_all.reshape(experts, TOP, sequence_length)
    else:
        full_qkv = gather_shards(local_qkv)
        full_out = gather_shards(w_out)
        small_all = lax.all_gather(small_flat, "fsdp", axis=0)
    small_parts = []
    offset = 0
    for array, size in zip(small, small_sizes):
        part = small_all[:, offset : offset + size]
        small_parts.append(part.reshape((planes * array.shape[0],) + array.shape[1:]))
        offset += size
    full_router, attn_gain, ffn_gain, query_gain, key_gain = small_parts

    if in_blocks:
        plane_experts = lax.axis_index("fsdp") * PLANE + jnp.arange(PLANE, dtype=jnp.int32)
        plane_hits = jnp.any(routes_all[None] == plane_experts[:, None, None, None], axis=2)
        positions = ranks(plane_hits)
    else:
        hits = jnp.any(routes[None, :, :] == expert_ids[:, None, None], axis=-1)
        select = places(hits, capacity)
        cot_rows = jnp.einsum("brt,td->brd", select, cotangent, preferred_element_type=f32)
        cot_rows = lax.all_to_all(cot_rows.astype(brain_float), BOTH, 0, 0, tiled=True)

    inputs = tokens.astype(f32)
    normalized, norm_attn_back = jax.vjp(root_mean_norm, inputs, attn_gain.astype(f32))
    normed_low = normalized.astype(brain_float)
    qkv_raw = jnp.dot(normed_low, full_qkv, preferred_element_type=f32)
    cosine, sine = rope_tables(sequence_length, HEAD_SIZE)
    head_gains = (query_gain.astype(f32)[None, :], key_gain.astype(f32)[None, :])
    mixed_low, query_rot, key_rot, value_low, totals = attention(
        qkv_raw, segments, cosine, sine, *head_gains
    )
    hidden = inputs + jnp.dot(mixed_low, full_out, preferred_element_type=f32)
    routed, norm_ffn_back = jax.vjp(root_mean_norm, hidden, ffn_gain.astype(f32))
    routed_low = routed.astype(brain_float)
    logits = jnp.dot(routed_low, full_router, preferred_element_type=f32)
    chosen_mask = jnp.any(routes[:, :, None] == expert_ids[None, None, :], axis=1)

    def gating(logit_in):
        softmax_probs = jax.nn.softmax(logit_in, axis=-1)
        chosen = jnp.where(chosen_mask, softmax_probs, 0.0)
        return chosen / jnp.sum(chosen, axis=-1, keepdims=True)

    gates, gating_back = jax.vjp(gating, logits)
    flat = (experts * capacity, MODEL_WIDTH)
    if in_blocks:
        (
            rows,
            cot_rows,
            out_rows,
            out_second,
            rows_grad,
            act_low,
            gate_low,
            up_low,
            gate_grad,
        ) = dispatch_and_expert(
            routed_low,
            cotangent,
            cot_line,
            cot_sides,
            positions,
            gates.T.reshape(GATE_SHAPE),
            w_gate[0],
            w_up[0],
            w_down[0],
            capacity,
            1,
        )
    else:
        rows = jnp.einsum("brt,td->brd", select, routed_low, preferred_element_type=f32)
        rows = lax.all_to_all(rows.astype(brain_float), BOTH, 0, 0, tiled=True)
        here = lax.all_to_all(select, BOTH, 0, 0, tiled=True)
        gates_here = lax.all_to_all(gates.T, BOTH, 0, 0, tiled=True)
        row_gates = jnp.sum(here.astype(f32) * gates_here[:, None, :], axis=-1)
        (
            out_rows,
            rows_grad,
            row_gate_grad,
            gate_weight_grad,
            up_weight_grad,
            down_weight_grad,
        ) = expert_layer(
            rows.reshape(flat),
            cot_rows.reshape(flat),
            row_gates.reshape(-1),
            w_gate[0],
            w_up[0],
            w_down[0],
        )
        row_gate_grad = row_gate_grad.reshape(experts, capacity, 1)
        gate_grad = jnp.sum(here.astype(f32) * row_gate_grad, axis=1)

    def exchange_back(block, select_here):
        block = block.reshape(experts, capacity, MODEL_WIDTH)
        block = lax.all_to_all(block, BOTH, 0, 0, tiled=True)
        return jnp.einsum("brt,brd->td", select_here, block, preferred_element_type=f32)

    if in_blocks:
        routed_grad, gate_grad = combine(
            rows_grad.reshape(experts, capacity, MODEL_WIDTH), positions, gate_grad, 2
        )
        gate_grad = gate_grad.reshape(experts, sequence_length).T
        (
            out_rows,
            rows,
            cot_rows,
            act_low,
            gate_low,
            up_low,
            routed_grad,
        ) = lax.optimization_barrier(
            (out_rows, rows, cot_rows, act_low, gate_low, up_low, routed_grad)
        )

        def in_plane(block):
            return lax.all_to_all(
                block.reshape(PLANE, LINE, capacity, -1), "expert", 0, 0, tiled=True
            )

        gate_weight_grad, up_weight_grad = routed_weight_grads(
            rows.reshape(flat), gate_low.reshape(flat[0], -1), up_low.reshape(flat[0], -1)
        )

        def in_plane(block):
            return lax.all_to_all(
                block.reshape(PLANE, LINE, capacity, -1), "expert", 0, 0, tiled=True
            )

        returned = in_plane(out_rows)
        line_positions = lax.dynamic_index_in_dim(
            positions.reshape(PLANE, LINE, PLANE, sequence_length),
            lax.axis_index("expert"),
            axis=2,
            keepdims=False,
        )
        slots = jnp.arange(capacity, dtype=jnp.int32)
        line_select = (line_positions[:, :, None, :] == slots[:, None]).astype(brain_float)

        def sum_along(block):
            sums = jnp.einsum("ezct,ezcd->ztd", line_select, block, preferred_element_type=f32)
            sums = sums.astype(brain_float).reshape(-1, block.shape[-1])
            return lax.psum_scatter(sums, "fsdp", scatter_dimension=0, tiled=True), sums

    else:
        gate_grad = lax.all_to_all(gate_grad, BOTH, 0, 0, tiled=True).T
        routed_grad = exchange_back(rows_grad, select)
        result = hidden + exchange_back(out_rows, select)
    upstream = cotangent.astype(f32)
    logit_low = gating_back(gate_grad)[0].astype(brain_float)
    routed_grad = routed_grad + jnp.einsum(
        "se,de->sd", logit_low, full_router, preferred_element_type=f32
    )
    router_grad = jnp.einsum("sd,se->de", routed_low, logit_low, preferred_element_type=f32)
    hidden_grad, ffn_gain_grad = norm_ffn_back(routed_grad)
    hidden_grad = hidden_grad + upstream
    hidden_low = hidden_grad.astype(brain_float)
    mixture_gradient = jnp.einsum(
        "sd,ad->sa", hidden_low, full_out, preferred_element_type=f32
    ).astype(brain_float)
    query_pre, key_pre, value_pre, gain_grads = attention_back(
        qkv_raw,
        query_rot,
        key_rot,
        value_low,
        mixture_gradient,
        totals,
        segments,
        cosine,
        sine,
        *head_gains,
    )
    if in_blocks:
        (
            returned,
            out_second,
            query_pre,
            gate_weight_grad,
            up_weight_grad,
            cot_rows,
            act_low,
            mixed_low,
        ) = lax.optimization_barrier(
            (
                returned,
                out_second,
                query_pre,
                gate_weight_grad,
                up_weight_grad,
                cot_rows,
                act_low,
                mixed_low,
            )
        )
        down_weight_grad = down_weight_grads(
            cot_rows.reshape(flat), act_low.reshape(flat[0], -1)
        )
        result_first, _ = sum_along(returned)
        returned = in_plane(out_second)
    out_grad = jnp.einsum("sa,sd->ad", mixed_low, hidden_low, preferred_element_type=f32)
    qkv_pre = jnp.concatenate([query_pre, key_pre, value_pre], axis=1)
    qkv_weight_grad = jnp.einsum("sd,sa->da", normed_low, qkv_pre, preferred_element_type=f32)
    normed_grad = jnp.einsum("sa,da->sd", qkv_pre, full_qkv, preferred_element_type=f32)
    input_grad, attn_gain_grad = norm_attn_back(normed_grad)
    input_grad = (input_grad + hidden_grad).astype(brain_float)
    small_grads = [
        grad.reshape(planes, -1).astype(brain_float)
        for grad in (router_grad, attn_gain_grad, ffn_gain_grad, gain_grads[0], gain_grads[1])
    ]
    small_grads = jnp.concatenate(small_grads, axis=1)
    if in_blocks:
        lanes = 128
        width = -(-small_grads.shape[1] // (PLANE * 32 * lanes)) * (PLANE * 32 * lanes)
        small_grads = jnp.pad(small_grads, ((0, 0), (0, width - small_grads.shape[1])))
        qkv_low = qkv_weight_grad.astype(brain_float)
        out_low = out_grad.astype(brain_float)
        (
            returned,
            qkv_low,
            out_low,
            input_grad,
            gate_weight_grad,
            up_weight_grad,
            down_weight_grad,
        ) = lax.optimization_barrier(
            (
                returned,
                qkv_low,
                out_low,
                input_grad,
                gate_weight_grad,
                up_weight_grad,
                down_weight_grad,
            )
        )
        result_second, expert_sums = sum_along(returned)
        qkv_low, expert_sums = lax.optimization_barrier((qkv_low, expert_sums))
        qkv_sum, out_sum, small_sums = reduce_all(
            (qkv_low, out_low, small_grads.reshape(-1, lanes)), 4
        )
        qkv_sum, out_sum = qkv_sum.astype(f32), out_sum.astype(f32)
        result = hidden + jnp.concatenate([result_first, result_second], axis=1).astype(f32)
        small_sums = small_sums.reshape(-1).astype(f32)
    else:
        qkv_sum = scatter_sums(qkv_weight_grad.astype(brain_float))
        out_sum = scatter_sums(out_grad.astype(brain_float))
        small_sums = lax.psum(
            lax.psum_scatter(small_grads, "fsdp", scatter_dimension=0, tiled=True), "expert"
        ).astype(f32)[0]
    query_width = QUERY_HEADS * HEAD_SIZE
    key_width = query_width + KEY_VALUE_HEADS * HEAD_SIZE
    summed = [
        qkv_sum[:, :query_width],
        qkv_sum[:, query_width:key_width],
        qkv_sum[:, key_width:],
        out_sum,
    ]
    offset = 0
    for array, size in zip(small, small_sizes):
        summed.append(small_sums[offset : offset + size].reshape(array.shape))
        offset += size
    return (
        (result.astype(brain_float), input_grad)
        + tuple(summed)
        + (gate_weight_grad[None], up_weight_grad[None], down_weight_grad[None])
    )


def solution(mesh):
    in_specs = (
        P(("fsdp", "expert"), None),
        P(("fsdp", "expert"), None),
        P(("fsdp", "expert"), None),
        P("fsdp", None),
        P("fsdp", None),
        P("fsdp", None),
        P("fsdp", None),
        P("fsdp", None),
        P("fsdp"),
        P("fsdp"),
        P("fsdp"),
        P("fsdp"),
        P(("fsdp", "expert"), None, None),
        P(("fsdp", "expert"), None, None),
        P(("fsdp", "expert"), None, None),
        P(("fsdp", "expert"), None),
    )
    out_specs = (
        P(("fsdp", "expert"), None),
        P(("fsdp", "expert"), None),
        P("fsdp", None),
        P("fsdp", None),
        P("fsdp", None),
        P("fsdp", None),
        P("fsdp", None),
        P("fsdp"),
        P("fsdp"),
        P("fsdp"),
        P("fsdp"),
        P(("fsdp", "expert"), None, None),
        P(("fsdp", "expert"), None, None),
        P(("fsdp", "expert"), None, None),
    )
    return jax.shard_map(
        on_device, mesh=mesh, in_specs=in_specs, out_specs=out_specs, check_vma=False
    )
```

time: 3830 us -> 1390 us (0.36)
  waiting for transfers between devices: 2190 us -> 19.1 us
  Pallas kernels: 0 us -> 1070 us
  blocking collectives: 515 us -> 0 us
  local copies, waits for them, and re-layouts: 385 us -> 34.1 us
  matrix products: 454 us -> 199 us
  other arithmetic: 193 us -> 31.9 us
  starting transfers between devices: 66 us -> 17.8 us
    all_to_all x4 -> x2, waiting for transfers between devices: 1110 us -> 19 us  [in_plane(): lax.all_to_all(block.reshape(PLANE, LINE, capacity, -1), 'expert', 0, 0,...]
    pallas_call x0 -> x6, Pallas kernels: none -> 1070 us  [the longest x1 366 us: dispatch_and_expert(): pl.pallas_call(expert_kernel, out_shape=[wide, wide, half_wide, half_wide...]
    all_gather x4 -> x0, waiting for transfers between devices: 502 us -> none  [the longest x1 282 us: on_device(): lax.all_gather(w_query, 'fsdp', axis=0, tiled=True)]
    reduce_scatter x5 -> x2, waiting for transfers between devices: 499 us -> 0.01 us  [sum_along(): lax.psum_scatter(sums, 'fsdp', scatter_dimension=0, tiled=True)]
    all_gather x3 -> x0, blocking collectives: 472 us -> none  [the longest x1 453 us: on_device(): lax.all_gather(w_router, 'fsdp', axis=0, tiled=True)]
    dot_general x23 -> x9, matrix products: 367 us -> 146 us  [the longest x2 44.5 us: routed_weight_grads(): jnp.einsum('rd,rf->df', rows, low, preferred_element_type=jnp.float32)]
    gather x4 -> x0, local copies, waits for them, and re-layouts: 170 us -> none  [the longest x1 46.8 us: on_device(): send_grads = padded_grads[source].reshape(experts, capacity, MODEL_WIDTH)]
    slice x4 -> x10, local copies, waits for them, and re-layouts: 150 us -> 12.3 us  [the longest x1 4.48 us: on_device(): qkv_sum[:, :query_width]]
  transfers between devices with their start and end apart: 14 -> 6, of which waited for: 9 -> 1; matrix products, arithmetic and copies ran while one was open for 17% -> 17% of each run, Pallas kernels for 0% -> 22%
where the time goes in v1:
time: 1390 us
  Pallas kernels  1070 us (77%)
  matrix products  199 us (14%)
  local copies, waits for them, and re-layouts  34.1 us (2%)
  other arithmetic  31.9 us (2%)
  waiting for transfers between devices  19.1 us (1%)
  starting transfers between devices  17.8 us (1%)
  between operations  15.4 us (1%)
    pallas_call x1, Pallas kernels, dispatch_and_expert(): pl.pallas_call(expert_kernel, out_shape=[wide, wide, half_wide, half_wide...  366 us
    pallas_call x1, Pallas kernels, combine(): pl.pallas_call(combine_kernel, out_shape=[jax.ShapeDtypeStruct((DEVICE_TO...  246 us
    pallas_call x1, Pallas kernels, reduce_all(): pl.pallas_call(functools.partial(reduce_kernel, len(arrays)), out_shape=[...  218 us
    pallas_call x1, Pallas kernels, gather_all(): pl.pallas_call(functools.partial(gather_kernel, kinds), out_shape=[jax.Sh...  157 us
    pallas_call x1, Pallas kernels, attention_back(): pl.pallas_call(attention_back_kernel, grid=(KEY_VALUE_HEADS,), in_specs=[...  45.8 us
    dot_general x2, matrix products, routed_weight_grads(): jnp.einsum('rd,rf->df', rows, low, preferred_element_type=jnp.float32)  44.5 us
    pallas_call x1, Pallas kernels, attention(): pl.pallas_call(attention_kernel, grid=(KEY_VALUE_HEADS,), in_specs=[pl.Bl...  34.8 us
  transfers between devices with their start and end apart: 6, of which 1 were waited for; matrix products, arithmetic and copies ran while one was open for 17% of the time, Pallas kernels for 22%

profile of v1, /device:TPU:11, one launch (start us, length us, event | category | flops | bytes accessed | tf_op | source)
XLA Modules:
  0.0 1385.4 jit_solution(1260783986641545300)
XLA Ops:
  7.2 1.4 fusion.44
  8.6 0.9 copy.52
  9.6 2.8 concatenate.25
  12.7 4.0 pad_maximum_fusion.refs_0_
  16.7 156.8 %shard_map.263 = (bf16[2048,5120]{1,0:T(8,128)(2,1)}, bf16[4096,2048]{1,0:T(8,128)(2,1)}, bf16[64,1152]{1,0:T(8,128)(2,1)S(1)}, bf16[2048,1024]{1,0:T(8,128)(2,1)S(1)}, s32[256,512]{1,0:T(8,128)S(1)}) custom-call(bf16[512,5120]{1,0:T(8,128)(2,1)S(1)} %pad_maximum_fusion.refs_0_, bf16[1024,2048]{1,0:T(8,128)(2,1)S(1)} %copy-done.1, ...), custom_call_target="tpu_custom_call" | custom-call | tf_op jit(solution)/shard_map/pallas_call | solution.py:721
  173.5 2.4 fusion.43
  175.9 1.1 copy-done
  177.2 1.2 collective-permute-start.1
  179.8 1.7 fusion.31
  181.7 17.7 %fusion.26.query_ref.key_ref.value_ref = f32[512,5120]{1,0:T(8,128)} fusion(bf16[2048,5120]{1,0:T(8,128)(2,1)} %get-tuple-element.66, bf16[512,2048]{1,0:T(8,128)(2,1)S(1)} %copy-done.20, f32[2048]{0:T(1024)S(1)} %bitcast.123, f32[512]{0:T(512)S(1)} %fusion.39), kind=kOutput, calls=%fused_computation.47 | convolution fusion | flops 10741612544 | bytes 33564672 | tf_op jit(solution)/shard_map/dot_general | solution.py:1915
  199.7 34.8 %shard_map.264 = (bf16[512,4096]{1,0:T(8,128)(2,1)}, bf16[512,4096]{1,0:T(8,128)(2,1)}, bf16[512,512]{1,0:T(8,128)(2,1)S(1)}, bf16[512,512]{1,0:T(8,128)(2,1)S(1)}, f32[4,512,8]{2,1,0:T(8,128)S(1)}) custom-call(f32[512,5120]{1,0:T(8,128)} %fusion.26.query_ref.key_ref.value_ref, f32[512,5120]{1,0:T(8,128)} %fusion.26.query_ref.key_ref.value_ref, ...), custom_call_target="tpu_custom_call" | custom-call | tf_op jit(solution)/shard_map/pallas_call | solution.py:1084
  234.5 13.9 %multiply_reduce_fusion.2 = (f32[512]{0:T(512)S(1)}, f32[512,2048]{1,0:T(8,128)S(1)}) fusion(bf16[512,4096]{1,0:T(8,128)(2,1)} %get-tuple-element.99, bf16[4096,2048]{1,0:T(8,128)(2,1)} %get-tuple-element.68, bf16[512,2048]{1,0:T(8,128)(2,1)S(1)} %copy-done.20), kind=kOutput, calls=%fused_computation.33 | convolution fusion | flops 8594128896 | bytes 27265024 | tf_op jit(solution)/shard_map/dot_general | solution.py:1921
  248.5 1.9 copy-done.12
  251.1 0.7 fusion.46
  252.1 0.7 reshape.212.gates_ref
  252.8 1.6 compare_reduce_fusion
  255.6 366.5 %shard_map.265 = (bf16[32,160,2048]{2,1,0:T(8,128)(2,1)}, bf16[32,160,2048]{2,1,0:T(8,128)(2,1)}, bf16[32,160,1024]{2,1,0:T(8,128)(2,1)}, bf16[32,160,1024]{2,1,...) custom-call(s32[8,32,512]{2,1,0:T(8,128)} %copy-done.24, ...), custom_call_target="tpu_custom_call" | custom-call | tf_op jit(solution)/shard_map/pallas_call | solution.py:1785
  622.1 245.8 %shard_map.266 = (f32[512,2048]{1,0:T(8,128)}, f32[4,8,1,512]{3,2,1,0:T(1,128)}) custom-call(s32[8,32,512]{2,1,0:T(8,128)} %copy-done.24, f32[4,8,1,512]{3,2,1,0:T(1,128)} %get-tuple-element.77.gate_grad_ref, bf16[32,160,2048]{2,1,0:T(8,128)(2,1)} %get-tuple-element.78.rows_ref), custom_call_target="tpu_custom_call" | custom-call | tf_op jit(solution)/shard_map/pallas_call | solution.py:450
  867.8 0.9 fusion.37
  868.7 0.9 multiply_reduce_fusion.3
  869.6 11.1 all-to-all-start
  880.8 7.6 multiply_reduce_fusion
  888.7 3.7 fusion.10
  892.4 15.4 %convolution_convert_fusion.2.mixed_grad_ref = bf16[512,4096]{1,0:T(8,128)(2,1)} fusion(bf16[4096,2048]{1,0:T(8,128)(2,1)} %get-tuple-element.68, f32[512,2048]{1,0:T(8,128)S(1)} %fusion.10), kind=kOutput, calls=%fused_computation.16 | convolution fusion | flops 8593080320 | bytes 25165824 | tf_op jit(solution)/shard_map/sd,ad->sa/dot_general | solution.py:2046
  907.8 45.8 %shard_map.267 = (bf16[512,4096]{1,0:T(8,128)(2,1)}, bf16[512,512]{1,0:T(8,128)(2,1)}, bf16[512,512]{1,0:T(8,128)(2,1)}, f32[8,128]{1,0:T(8,128)}) custom-call(f32[512,5120]{1,0:T(8,128)} %fusion.26.query_ref.key_ref.value_ref, f32[512,5120]{1,0:T(8,128)} %fusion.26.query_ref.key_ref.value_ref, bf16[512,4096]{1,0:T(8,128)(2,1)} %get-tuple-element.82.query_rot_ref, ...), custom_call_target="tpu_custom_call" | custom-call | tf_op jit(solution)/shard_map/pallas_call | solution.py:1204
  953.6 23.7 %convolution_bitcast_fusion.1 = f32[2048,768]{1,0:T(8,128)} fusion(bf16[32,160,2048]{2,1,0:T(8,128)(2,1)} %get-tuple-element.89, bf16[32,160,768]{2,1,0:T(8,128)(2,1)} %get-tuple-element.91), kind=kOutput, calls=%fused_computation.36 | convolution fusion | flops 16106127360 | bytes 35127296 | tf_op jit(solution)/shard_map/rd,rf->df/dot_general | solution.py:61
  977.4 20.8 %convolution_bitcast_fusion.2 = f32[2048,768]{1,0:T(8,128)} fusion(bf16[32,160,2048]{2,1,0:T(8,128)(2,1)} %get-tuple-element.89, bf16[32,160,768]{2,1,0:T(8,128)(2,1)S(1)} %bitcast.128), kind=kOutput, calls=%fused_computation.37 | convolution fusion | flops 16106127360 | bytes 35127296 | tf_op jit(solution)/shard_map/rd,rf->df/dot_general | solution.py:61
  998.2 4.7 constant_dynamic-update-slice_fusion.2
  1002.9 5.1 all-to-all-start.1
  1008.1 11.2 bitcast_convert_fusion.1
  1019.3 0.9 copy-done.34
  1020.3 0.8 constant_dynamic-update-slice_fusion.1
  1021.1 0.8 constant_dynamic-update-slice_fusion
  1021.9 19.7 %fusion.9 = (bf16[2048]{0:T(1024)(128)(2,1)S(1)}, f32[512]{0:T(512)S(1)}, f32[512,2048]{1,0:T(8,128)}) fusion(bf16[512,2048]{1,0:T(8,128)(2,1)S(1)} %copy-done.21, f32[512]{0:T(512)S(1)} %copy-done.52, f32[2048]{0:T(1024)S(1)} %bitcast.124, bf16[512,5120]{1,0:T(8,128)(2,1)} %constant_dynamic-update-slice_fusion, bf16[2048,5120]{1,0:T(8,128)(2,1)} %get-tuple-element.66), kind=kOutput, calls=%fused_computation.23 | convolution fusion | flops 10744756224 | bytes 32522240 | tf_op jit(solution)/shard_map/sa,da->sd/dot_general | solution.py:2091
  1041.6 6.0 fusion.12
  1047.6 18.3 %convolution_convert_fusion.refs_0_ = bf16[2048,5120]{1,0:T(8,128)(2,1)} fusion(bf16[512,5120]{1,0:T(8,128)(2,1)} %constant_dynamic-update-slice_fusion, bf16[512,2048]{1,0:T(8,128)(2,1)} %param.16, f32[2048]{0:T(1024)S(1)} %bitcast.126, f32[512]{0:T(512)S(1)} %copy-done.52), kind=kOutput, calls=%fused_computation | convolution fusion | flops 10752098304 | bytes 28321792 | tf_op jit(solution)/shard_map/sd,sa->da/dot_general | solution.py:2090
  1065.9 15.0 %convolution_convert_fusion.1.refs_1_ = bf16[4096,2048]{1,0:T(8,128)(2,1)} fusion(bf16[512,4096]{1,0:T(8,128)(2,1)} %get-tuple-element.99, f32[512,2048]{1,0:T(8,128)S(1)} %copy-done.17), kind=kOutput, calls=%fused_computation.1 | convolution fusion | flops 8599371776 | bytes 25165824 | tf_op jit(solution)/shard_map/sa,sd->ad/dot_general | solution.py:2088
  1080.9 23.1 %convolution_bitcast_fusion = f32[768,2048]{1,0:T(8,128)} fusion(bf16[32,160,768]{2,1,0:T(8,128)(2,1)} %get-tuple-element.102, bf16[32,160,2048]{2,1,0:T(8,128)(2,1)} %get-tuple-element.103), kind=kOutput, calls=%fused_computation.35 | convolution fusion | flops 16106127360 | bytes 35127296 | tf_op jit(solution)/shard_map/rf,rd->fd/dot_general | solution.py:67
  1104.0 19.0 %all-to-all-done.1 = bf16[8,4,160,1024]{3,2,1,0:T(8,128)(2,1)} async-done(((bf16[8,4,160,1024]{3,2,1,0:T(8,128)(2,1)}), bf16[8,4,160,1024]{3,2,1,0:T(8,128)(2,1)}, u32[]{:S(2)}, u32[]{:S(2)}) %all-to-all-start.1) | async-done | bytes 10485792 | tf_op jit(solution)/shard_map/all_to_all | solution.py:2014
  1123.0 11.2 bitcast_convert_fusion
  1134.3 1.5 copy-done.15
  1137.7 1.0 reshape.219.refs_2_
  1138.7 218.5 %shard_map.268 = (bf16[512,5120]{1,0:T(8,128)(2,1)}, bf16[1024,2048]{1,0:T(8,128)(2,1)}, bf16[256,128]{1,0:T(8,128)(2,1)}) custom-call(bf16[2048,5120]{1,0:T(8,128)(2,1)} %convolution_convert_fusion.refs_0_, bf16[4096,2048]{1,0:T(8,128)(2,1)} %convolution_convert_fusion.1.refs_1_, bf16[1024,128]{1,0:T(8,128)(2,1)} %reshape.219.refs_2_), custom_call_target="tpu_custom_call" | custom-call | tf_op jit(solution)/shard_map/pallas_call | solution.py:980
  1357.2 6.8 convert_element_type.170
  1364.0 4.5 slice.103
  1368.6 0.7 copy.59
  1370.5 2.8 fusion.42
  1373.3 4.8 add_convert_fusion
  (175 shorter events, 8.0 us)
Async XLA Ops:
  7.2 5.4 copy-start.32
  7.2 5.4 copy-start.31
  12.6 4.0 copy-start.1
  12.7 4.0 copy-start.8
  173.5 3.4 copy-start
  173.5 5.1 copy-start.20
  173.5 8.0 copy-start.9
  176.9 78.0 %collective-permute-start = (bf16[4,512,512]{2,1,0:T(8,128)(2,1)}, bf16[4,512,512]{2,1,0:T(8,128)(2,1)}, u32[]{:S(2)}, u32[]{:S(2)}) collective-permute-start(bf16[4,512,512]{2,1,0:T(8,128)(2,1)} %get-tuple-element.181), channel_id=1, source_target_pairs={{0,2},{1,3},{2,0},{3,1},{4,6},{5,7},{6,4},{7,5},{8,10},{9,11},{10,... | collective-permute-start | bytes 6291464 | tf_op jit(solution)/shard_map/ppermute | solution.py:1881
  177.2 77.7 %collective-permute-start.1 = (bf16[4,512,512]{2,1,0:T(8,128)(2,1)}, bf16[4,512,512]{2,1,0:T(8,128)(2,1)}, u32[]{:S(2)}, u32[]{:S(2)}) collective-permute-start(bf16[4,512,512]{2,1,0:T(8,128)(2,1)} %get-tuple-element.180), channel_id=1, source_target_pairs={{0,4},{1,5},{2,6},{3,7},{4,0},{5,1},{6,2},{7,3},{8,12},{9,13},{10,... | collective-permute-start | bytes 6291464 | tf_op jit(solution)/shard_map/ppermute | solution.py:1881
  178.6 20.8 %copy-start.42 = (f32[1,4,4,128]{3,1,2,0:T(4,128)}, f32[1,4,4,128]{3,1,2,0:T(4,128)S(1)}, u32[]{:S(2)}) copy-start(f32[1,4,4,128]{3,1,2,0:T(4,128)S(1)} %copy.64) | copy-start | bytes 24580
  179.7 19.8 %copy-start.51 = (f32[512]{0:T(512)}, f32[512]{0:T(512)S(1)}, u32[]{:S(2)}) copy-start(f32[512]{0:T(512)S(1)} %fusion.39) | copy-start | bytes 6148
  179.7 19.9 %copy-start.10 = (f32[1,128]{1,0:T(1,128)}, f32[1,128]{1,0:T(1,128)S(1)}, u32[]{:S(2)}) copy-start(f32[1,128]{1,0:T(1,128)S(1)} %reshape.221.query_gain_ref) | copy-start | bytes 1540
  179.8 19.8 %copy-start.11 = (f32[1,128]{1,0:T(1,128)}, f32[1,128]{1,0:T(1,128)S(1)}, u32[]{:S(2)}) copy-start(f32[1,128]{1,0:T(1,128)S(1)} %reshape.222.key_gain_ref) | copy-start | bytes 1540
  181.7 18.0 %copy-start.4 = (s32[512,1]{1,0:T(8,128)}, s32[512,1]{1,0:T(8,128)S(1)}, u32[]{:S(2)}) copy-start(s32[512,1]{1,0:T(8,128)S(1)} %copy.53.column_ref) | copy-start | bytes 6148
  181.7 17.7 %copy-start.27 = (f32[512,64]{1,0:T(8,128)S(1)}, f32[512,64]{1,0:T(8,128)}, u32[]{:S(2)}) copy-start(f32[512,64]{1,0:T(8,128)} %get-tuple-element.196) | copy-start | bytes 393220
  199.6 34.9 %copy-start.2 = (f32[512,128]{1,0:T(8,128)}, f32[512,128]{1,0:T(8,128)S(1)}, u32[]{:S(2)}) copy-start(f32[512,128]{1,0:T(8,128)S(1)} %get-tuple-element.203.cosine_ref) | copy-start | bytes 786436
  199.7 34.9 %copy-start.3 = (f32[512,128]{1,0:T(8,128)}, f32[512,128]{1,0:T(8,128)S(1)}, u32[]{:S(2)}) copy-start(f32[512,128]{1,0:T(8,128)S(1)} %get-tuple-element.204.sine_ref) | copy-start | bytes 786436
  234.5 13.9 %copy-start.5 = (f32[4,512,8]{2,1,0:T(8,128)}, f32[4,512,8]{2,1,0:T(8,128)S(1)}, u32[]{:S(2)}) copy-start(f32[4,512,8]{2,1,0:T(8,128)S(1)} %get-tuple-element.87.total_ref) | copy-start | bytes 196612
  234.5 13.9 %copy-start.6 = (bf16[512,512]{1,0:T(8,128)(2,1)}, bf16[512,512]{1,0:T(8,128)(2,1)S(1)}, u32[]{:S(2)}) copy-start(bf16[512,512]{1,0:T(8,128)(2,1)S(1)} %get-tuple-element.83.key_rot_ref) | copy-start | bytes 1572868
  234.5 13.9 %copy-start.7 = (bf16[512,512]{1,0:T(8,128)(2,1)}, bf16[512,512]{1,0:T(8,128)(2,1)S(1)}, u32[]{:S(2)}) copy-start(bf16[512,512]{1,0:T(8,128)(2,1)S(1)} %get-tuple-element.84.value_ref) | copy-start | bytes 1572868
  250.8 4.1 copy-start.14
  251.9 628.8 %copy-start.22 = (f32[512,32]{0,1:T(8,128)}, f32[512,32]{0,1:T(8,128)S(1)}, u32[]{:S(2)}) copy-start(f32[512,32]{0,1:T(8,128)S(1)} %get-tuple-element.200) | copy-start | bytes 196612
  251.9 628.8 %copy-start.36 = (f32[512]{0:T(512)}, f32[512]{0:T(512)S(1)}, u32[]{:S(2)}) copy-start(f32[512]{0:T(512)S(1)} %get-tuple-element.199) | copy-start | bytes 6148
  251.9 628.8 %copy-start.38 = (f32[512]{0:T(512)}, f32[512]{0:T(512)S(1)}, u32[]{:S(2)}) copy-start(f32[512]{0:T(512)S(1)} %fusion.38) | copy-start | bytes 6148
  252.0 628.7 %copy-start.28 = (pred[512,32]{0,1:T(8,128)(4,1)}, pred[512,32]{0,1:T(8,128)(4,1)S(1)}, u32[]{:S(2)}) copy-start(pred[512,32]{0,1:T(8,128)(4,1)S(1)} %fusion.28) | copy-start | bytes 49156
  252.1 628.7 %copy-start.40 = (f32[512]{0:T(512)}, f32[512]{0:T(512)S(1)}, u32[]{:S(2)}) copy-start(f32[512]{0:T(512)S(1)} %fusion.41) | copy-start | bytes 6148
  868.7 12.1 copy-start.44
  869.6 11.2 copy-start.48
  869.6 11.2 copy-start.25
  869.6 128.5 %all-to-all-start = ((bf16[8,4,160,1024]{3,2,1,0:T(8,128)(2,1)}), bf16[8,4,160,1024]{3,2,1,0:T(8,128)(2,1)}, u32[]{:S(2)}, u32[]{:S(2)}) async-start(bf16[8,4,160,1024]{3,2,1,0:T(8,128)(2,1)} %bitcast.111), calls=%async_computation | async-start | bytes 20971520 | tf_op jit(solution)/shard_map/all_to_all | solution.py:2014
  880.8 7.6 copy-start.13
  880.8 7.6 copy-start.18
  880.8 7.9 copy-start.19
  892.4 15.4 %copy-start.16 = (f32[512,2048]{1,0:T(8,128)}, f32[512,2048]{1,0:T(8,128)S(1)}, u32[]{:S(2)}) copy-start(f32[512,2048]{1,0:T(8,128)S(1)} %fusion.10) | copy-start | bytes 12582916
  907.8 69.6 %slice-start.3 = ((s8[7864320]{0:T(1024)(128)(4,1)}), s8[3670016]{0:T(1024)(128)(4,1)S(1)}, s32[]{:S(2)}) async-start(s8[7864320]{0:T(1024)(128)(4,1)} %bitcast.127), calls=%async_computation.9 | async-start | bytes 7340032
  953.6 23.8 %slice-start.4 = ((s8[7864320]{0:T(1024)(128)(4,1)}), s8[4194304]{0:T(1024)(128)(4,1)S(1)}, s32[]{:S(2)}) async-start(s8[7864320]{0:T(1024)(128)(4,1)} %bitcast.127), calls=%async_computation.10 | async-start | bytes 8388608
  1002.9 120.1 %all-to-all-start.1 = ((bf16[8,4,160,1024]{3,2,1,0:T(8,128)(2,1)}), bf16[8,4,160,1024]{3,2,1,0:T(8,128)(2,1)}, u32[]{:S(2)}, u32[]{:S(2)}) async-start(bf16[8,4,160,1024]{3,2,1,0:T(8,128)(2,1)} %bitcast.110), calls=%async_computation.2 | async-start | bytes 20971520 | tf_op jit(solution)/shard_map/all_to_all | solution.py:2014
  1008.0 365.3 %reduce-scatter.3.cloned.1.call-start = ((), (), s32[]{:S(2)}) async-start(), calls=%async_computation.4 | async-start | bytes 5242880 | tf_op jit(solution)/shard_map/reduce_scatter | solution.py:2031
  1019.2 2.7 copy-start.21
  1019.2 2.7 copy-start.43
  1019.3 354.1 %reduce-scatter.5.cloned.1.call-start = ((), (), s32[]{:S(2)}) async-start(), calls=%async_computation.5 | async-start | bytes 5242880 | tf_op jit(solution)/shard_map/reduce_scatter | solution.py:2031
  1021.9 19.7 %copy-start.47 = (f32[512]{0:T(512)S(1)}, f32[512]{0:T(512)}, u32[]{:S(2)}) copy-start(f32[512]{0:T(512)} %copy-done.46) | copy-start | bytes 6148
  1047.6 18.3 %copy-start.17 = (f32[512,2048]{1,0:T(8,128)S(1)}, f32[512,2048]{1,0:T(8,128)}, u32[]{:S(2)}) copy-start(f32[512,2048]{1,0:T(8,128)} %copy-done.16) | copy-start | bytes 12582916
  1134.3 2.9 copy-start.53
  1134.3 3.1 copy-start.50
  1357.1 6.8 slice-start
  1357.1 6.8 slice-start.1
  1364.0 4.5 copy-start.35
  (17 other events, 26.9 us)
Sparse Core Ops, SparseCore 0:
  1019.4 75.5 reduce-scatter.2
  1134.5 86.9 reduce-scatter.4

commit v2 on v1

--- a/solution.py
+++ b/solution.py
@@ -1246,6 +1246,7 @@
 
 
 UNITS = 16
+FIRST_COLUMNS = 1152
 GATE_SHAPE = (LINE, PLANE, 1, DEVICE_TOKENS)
 LAG = 4
 CHUNK = 2
@@ -1586,8 +1587,11 @@
             at = pl.ds(number * capacity, capacity)
             for kind, (held, goal) in enumerate(
                 (
-                    (out_held.at[:, pl.ds(0, MODEL_WIDTH // 2)], out_ref),
-                    (out_held.at[:, pl.ds(MODEL_WIDTH // 2, MODEL_WIDTH // 2)], out_second_ref),
+                    (out_held.at[:, pl.ds(0, FIRST_COLUMNS)], out_ref),
+                    (
+                        out_held.at[:, pl.ds(FIRST_COLUMNS, MODEL_WIDTH - FIRST_COLUMNS)],
+                        out_second_ref,
+                    ),
                     (back_held, back_ref),
                     (act_held, act_ref),
                     (gate_held, gate_low_ref),
@@ -1776,7 +1780,6 @@
     blocks = LINE * PLANE
     dma = pltpu.SemaphoreType.DMA
     wide = jax.ShapeDtypeStruct((blocks, capacity, MODEL_WIDTH), low)
-    half_wide = jax.ShapeDtypeStruct((blocks, capacity, MODEL_WIDTH // 2), low)
     narrow = jax.ShapeDtypeStruct((blocks, capacity, w_gate.shape[1]), low)
     landing = jax.ShapeDtypeStruct((2, 2, LINE, 2, DEVICE_TOKENS, PART), low)
     vmem = pl.BlockSpec(memory_space=pltpu.VMEM)
@@ -1787,8 +1790,8 @@
         out_shape=[
             wide,
             wide,
-            half_wide,
-            half_wide,
+            jax.ShapeDtypeStruct((blocks, capacity, FIRST_COLUMNS), low),
+            jax.ShapeDtypeStruct((blocks, capacity, MODEL_WIDTH - FIRST_COLUMNS), low),
             wide,
             narrow,
             narrow,

time: 1390 us -> 1390 us (level)
  transfers between devices with their start and end apart: 6 -> 6, of which waited for: 1 -> 2; matrix products, arithmetic and copies ran while one was open for 17% -> 17% of each run, Pallas kernels for 22% -> 22%
where the time goes in v2:
time: 1390 us; the launch traced here: 1380 us
  Pallas kernels  1070 us (77%)
  matrix products  203 us (15%)
  other arithmetic  32.3 us (2%)
  local copies, waits for them, and re-layouts  30.7 us (2%)
  starting transfers between devices  19.3 us (1%)
  between operations  15.4 us (1%)
  waiting for transfers between devices  14.7 us (1%)
    pallas_call x1, Pallas kernels, dispatch_and_expert(): pl.pallas_call(expert_kernel, out_shape=[wide, wide, jax.ShapeDtypeStruct...  366 us
    pallas_call x1, Pallas kernels, combine(): pl.pallas_call(combine_kernel, out_shape=[jax.ShapeDtypeStruct((DEVICE_TO...  246 us
    pallas_call x1, Pallas kernels, reduce_all(): pl.pallas_call(functools.partial(reduce_kernel, len(arrays)), out_shape=[...  219 us
    pallas_call x1, Pallas kernels, gather_all(): pl.pallas_call(functools.partial(gather_kernel, kinds), out_shape=[jax.Sh...  157 us
    pallas_call x1, Pallas kernels, attention_back(): pl.pallas_call(attention_back_kernel, grid=(KEY_VALUE_HEADS,), in_specs=[...  45.9 us
    dot_general x2, matrix products, routed_weight_grads(): jnp.einsum('rd,rf->df', rows, low, preferred_element_type=jnp.float32)  44.5 us
    pallas_call x1, Pallas kernels, attention(): pl.pallas_call(attention_kernel, grid=(KEY_VALUE_HEADS,), in_specs=[pl.Bl...  34.8 us
  transfers between devices with their start and end apart: 6, of which 2 were waited for; matrix products, arithmetic and copies ran while one was open for 17% of the time, Pallas kernels for 22%

profile of v2, /device:TPU:11, one launch (start us, length us, event | category | flops | bytes accessed | tf_op | source)
XLA Modules:
  0.0 1383.5 jit_solution(338979059959155211)
XLA Ops:
  7.2 1.4 fusion.44
  8.6 0.9 copy.52
  9.6 2.8 concatenate.25
  12.7 4.0 pad_maximum_fusion.refs_0_
  16.7 156.8 %shard_map.263 = (bf16[2048,5120]{1,0:T(8,128)(2,1)}, bf16[4096,2048]{1,0:T(8,128)(2,1)}, bf16[64,1152]{1,0:T(8,128)(2,1)S(1)}, bf16[2048,1024]{1,0:T(8,128)(2,1)S(1)}, s32[256,512]{1,0:T(8,128)S(1)}) custom-call(bf16[512,5120]{1,0:T(8,128)(2,1)S(1)} %pad_maximum_fusion.refs_0_, bf16[1024,2048]{1,0:T(8,128)(2,1)S(1)} %copy-done.1, ...), custom_call_target="tpu_custom_call" | custom-call | tf_op jit(solution)/shard_map/pallas_call | solution.py:721
  173.5 2.4 fusion.43
  175.9 1.1 copy-done
  177.2 1.2 collective-permute-start.1
  179.8 1.7 fusion.31
  181.7 17.8 %fusion.26.query_ref.key_ref.value_ref = f32[512,5120]{1,0:T(8,128)} fusion(bf16[2048,5120]{1,0:T(8,128)(2,1)} %get-tuple-element.66, bf16[512,2048]{1,0:T(8,128)(2,1)S(1)} %copy-done.19, f32[2048]{0:T(1024)S(1)} %bitcast.123, f32[512]{0:T(512)S(1)} %fusion.39), kind=kOutput, calls=%fused_computation.47 | convolution fusion | flops 10741612544 | bytes 33564672 | tf_op jit(solution)/shard_map/dot_general | solution.py:1918
  199.7 34.8 %shard_map.264 = (bf16[512,4096]{1,0:T(8,128)(2,1)}, bf16[512,4096]{1,0:T(8,128)(2,1)}, bf16[512,512]{1,0:T(8,128)(2,1)S(1)}, bf16[512,512]{1,0:T(8,128)(2,1)S(1)}, f32[4,512,8]{2,1,0:T(8,128)S(1)}) custom-call(f32[512,5120]{1,0:T(8,128)} %fusion.26.query_ref.key_ref.value_ref, f32[512,5120]{1,0:T(8,128)} %fusion.26.query_ref.key_ref.value_ref, ...), custom_call_target="tpu_custom_call" | custom-call | tf_op jit(solution)/shard_map/pallas_call | solution.py:1084
  234.6 16.2 %multiply_reduce_fusion.2 = (f32[512]{0:T(512)S(1)}, f32[512,2048]{1,0:T(8,128)}) fusion(bf16[512,4096]{1,0:T(8,128)(2,1)} %get-tuple-element.99, bf16[4096,2048]{1,0:T(8,128)(2,1)} %get-tuple-element.68, bf16[512,2048]{1,0:T(8,128)(2,1)S(1)} %copy-done.19), kind=kOutput, calls=%fused_computation.33 | convolution fusion | flops 8594128896 | bytes 27265024 | tf_op jit(solution)/shard_map/dot_general | solution.py:1924
  251.1 2.6 multiply_convert_fusion.routed_ref
  253.8 0.7 fusion.46
  254.7 0.7 reshape.212.gates_ref
  255.4 1.6 compare_reduce_fusion
  257.5 0.7 copy-done.23
  258.2 366.5 %shard_map.265 = (bf16[32,160,2048]{2,1,0:T(8,128)(2,1)}, bf16[32,160,2048]{2,1,0:T(8,128)(2,1)}, bf16[32,160,1152]{2,1,0:T(8,128)(2,1)}, bf16[32,160,896]{2,1,0...) custom-call(s32[8,32,512]{2,1,0:T(8,128)} %copy-done.23, ...), custom_call_target="tpu_custom_call" | custom-call | tf_op jit(solution)/shard_map/pallas_call | solution.py:1788
  624.7 245.6 %shard_map.266 = (f32[512,2048]{1,0:T(8,128)}, f32[4,8,1,512]{3,2,1,0:T(1,128)}) custom-call(s32[8,32,512]{2,1,0:T(8,128)} %copy-done.23, f32[4,8,1,512]{3,2,1,0:T(1,128)} %get-tuple-element.77.gate_grad_ref, bf16[32,160,2048]{2,1,0:T(8,128)(2,1)} %get-tuple-element.78.rows_ref), custom_call_target="tpu_custom_call" | custom-call | tf_op jit(solution)/shard_map/pallas_call | solution.py:450
  870.3 11.1 all-to-all-start
  881.7 7.6 multiply_reduce_fusion
  889.5 3.7 fusion.12
  893.2 15.4 %convolution_convert_fusion.2.mixed_grad_ref = bf16[512,4096]{1,0:T(8,128)(2,1)} fusion(bf16[4096,2048]{1,0:T(8,128)(2,1)} %get-tuple-element.68, f32[512,2048]{1,0:T(8,128)S(1)} %fusion.12), kind=kOutput, calls=%fused_computation.16 | convolution fusion | flops 8593080320 | bytes 25165824 | tf_op jit(solution)/shard_map/sd,ad->sa/dot_general | solution.py:2049
  908.6 45.9 %shard_map.267 = (bf16[512,4096]{1,0:T(8,128)(2,1)}, bf16[512,512]{1,0:T(8,128)(2,1)}, bf16[512,512]{1,0:T(8,128)(2,1)}, f32[8,128]{1,0:T(8,128)}) custom-call(f32[512,5120]{1,0:T(8,128)} %fusion.26.query_ref.key_ref.value_ref, f32[512,5120]{1,0:T(8,128)} %fusion.26.query_ref.key_ref.value_ref, bf16[512,4096]{1,0:T(8,128)(2,1)} %get-tuple-element.82.query_rot_ref, ...), custom_call_target="tpu_custom_call" | custom-call | tf_op jit(solution)/shard_map/pallas_call | solution.py:1204
  954.5 23.7 %convolution_bitcast_fusion.1 = f32[2048,768]{1,0:T(8,128)} fusion(bf16[32,160,2048]{2,1,0:T(8,128)(2,1)} %get-tuple-element.89, bf16[32,160,768]{2,1,0:T(8,128)(2,1)} %get-tuple-element.91), kind=kOutput, calls=%fused_computation.36 | convolution fusion | flops 16106127360 | bytes 35127296 | tf_op jit(solution)/shard_map/rd,rf->df/dot_general | solution.py:61
  978.3 20.8 %convolution_bitcast_fusion.2 = f32[2048,768]{1,0:T(8,128)} fusion(bf16[32,160,2048]{2,1,0:T(8,128)(2,1)} %get-tuple-element.89, bf16[32,160,768]{2,1,0:T(8,128)(2,1)S(1)} %bitcast.128), kind=kOutput, calls=%fused_computation.37 | convolution fusion | flops 16106127360 | bytes 35127296 | tf_op jit(solution)/shard_map/rd,rf->df/dot_general | solution.py:61
  999.1 11.4 all-to-all-done
  1010.5 4.7 constant_dynamic-update-slice_fusion.2
  1015.2 6.6 all-to-all-start.1
  1021.8 13.1 bitcast_convert_fusion
  1035.0 0.9 copy-done.33
  1036.0 0.8 constant_dynamic-update-slice_fusion.1
  1036.8 0.8 constant_dynamic-update-slice_fusion
  1037.6 19.6 %fusion.11 = (bf16[2048]{0:T(1024)(128)(2,1)S(1)}, f32[512]{0:T(512)S(1)}, f32[512,2048]{1,0:T(8,128)}) fusion(bf16[512,2048]{1,0:T(8,128)(2,1)S(1)} %copy-done.20, f32[512]{0:T(512)S(1)} %copy-done.51, f32[2048]{0:T(1024)S(1)} %bitcast.124, bf16[512,5120]{1,0:T(8,128)(2,1)} %constant_dynamic-update-slice_fusion, bf16[2048,5120]{1,0:T(8,128)(2,1)} %get-tuple-element.66), kind=kOutput, calls=%fused_computation.23 | convolution fusion | flops 10744756224 | bytes 32522240 | tf_op jit(solution)/shard_map/sa,da->sd/dot_general | solution.py:2094
  1057.3 5.9 fusion.14
  1063.2 18.3 %convolution_convert_fusion.refs_0_ = bf16[2048,5120]{1,0:T(8,128)(2,1)} fusion(bf16[512,5120]{1,0:T(8,128)(2,1)} %constant_dynamic-update-slice_fusion, bf16[512,2048]{1,0:T(8,128)(2,1)} %param.16, f32[2048]{0:T(1024)S(1)} %bitcast.126, f32[512]{0:T(512)S(1)} %copy-done.51), kind=kOutput, calls=%fused_computation | convolution fusion | flops 10752098304 | bytes 28321792 | tf_op jit(solution)/shard_map/sd,sa->da/dot_general | solution.py:2093
  1081.5 14.9 %convolution_convert_fusion.1.refs_1_ = bf16[4096,2048]{1,0:T(8,128)(2,1)} fusion(bf16[512,4096]{1,0:T(8,128)(2,1)} %get-tuple-element.99, f32[512,2048]{1,0:T(8,128)S(1)} %copy-done.16), kind=kOutput, calls=%fused_computation.1 | convolution fusion | flops 8599371776 | bytes 25165824 | tf_op jit(solution)/shard_map/sa,sd->ad/dot_general | solution.py:2091
  1096.4 23.1 %convolution_bitcast_fusion = f32[768,2048]{1,0:T(8,128)} fusion(bf16[32,160,768]{2,1,0:T(8,128)(2,1)} %get-tuple-element.102, bf16[32,160,2048]{2,1,0:T(8,128)(2,1)} %get-tuple-element.103), kind=kOutput, calls=%fused_computation.35 | convolution fusion | flops 16106127360 | bytes 35127296 | tf_op jit(solution)/shard_map/rf,rd->fd/dot_general | solution.py:67
  1119.6 3.2 all-to-all-done.1
  1122.8 10.9 bitcast_convert_fusion.1
  1135.6 1.0 reshape.219.refs_2_
  1136.6 218.6 %shard_map.268 = (bf16[512,5120]{1,0:T(8,128)(2,1)}, bf16[1024,2048]{1,0:T(8,128)(2,1)}, bf16[256,128]{1,0:T(8,128)(2,1)}) custom-call(bf16[2048,5120]{1,0:T(8,128)(2,1)} %convolution_convert_fusion.refs_0_, bf16[4096,2048]{1,0:T(8,128)(2,1)} %convolution_convert_fusion.1.refs_1_, bf16[1024,128]{1,0:T(8,128)(2,1)} %reshape.219.refs_2_), custom_call_target="tpu_custom_call" | custom-call | tf_op jit(solution)/shard_map/pallas_call | solution.py:980
  1355.2 6.8 convert_element_type.170
  1362.1 4.5 slice.103
  1366.7 0.7 copy.59
  1368.0 0.6 slice_bitcast_fusion
  1368.6 2.8 fusion.42
  1371.4 4.8 add_convert_fusion
  (173 shorter events, 6.4 us)
Async XLA Ops:
  7.2 5.4 copy-start.31
  7.2 5.4 copy-start.30
  173.5 8.0 copy-start.9
  176.9 80.6 %collective-permute-start = (bf16[4,512,512]{2,1,0:T(8,128)(2,1)}, bf16[4,512,512]{2,1,0:T(8,128)(2,1)}, u32[]{:S(2)}, u32[]{:S(2)}) collective-permute-start(bf16[4,512,512]{2,1,0:T(8,128)(2,1)} %get-tuple-element.181), channel_id=1, source_target_pairs={{0,2},{1,3},{2,0},{3,1},{4,6},{5,7},{6,4},{7,5},{8,10},{9,11},{10,... | collective-permute-start | bytes 6291464 | tf_op jit(solution)/shard_map/ppermute | solution.py:1884
  177.2 80.3 %collective-permute-start.1 = (bf16[4,512,512]{2,1,0:T(8,128)(2,1)}, bf16[4,512,512]{2,1,0:T(8,128)(2,1)}, u32[]{:S(2)}, u32[]{:S(2)}) collective-permute-start(bf16[4,512,512]{2,1,0:T(8,128)(2,1)} %get-tuple-element.180), channel_id=1, source_target_pairs={{0,4},{1,5},{2,6},{3,7},{4,0},{5,1},{6,2},{7,3},{8,12},{9,13},{10,... | collective-permute-start | bytes 6291464 | tf_op jit(solution)/shard_map/ppermute | solution.py:1884
  178.6 20.9 %copy-start.41 = (f32[1,4,4,128]{3,1,2,0:T(4,128)}, f32[1,4,4,128]{3,1,2,0:T(4,128)S(1)}, u32[]{:S(2)}) copy-start(f32[1,4,4,128]{3,1,2,0:T(4,128)S(1)} %copy.64) | copy-start | bytes 24580
  179.7 19.8 %copy-start.50 = (f32[512]{0:T(512)}, f32[512]{0:T(512)S(1)}, u32[]{:S(2)}) copy-start(f32[512]{0:T(512)S(1)} %fusion.39) | copy-start | bytes 6148
  179.7 20.0 %copy-start.10 = (f32[1,128]{1,0:T(1,128)}, f32[1,128]{1,0:T(1,128)S(1)}, u32[]{:S(2)}) copy-start(f32[1,128]{1,0:T(1,128)S(1)} %reshape.221.query_gain_ref) | copy-start | bytes 1540
  179.8 19.9 %copy-start.11 = (f32[1,128]{1,0:T(1,128)}, f32[1,128]{1,0:T(1,128)S(1)}, u32[]{:S(2)}) copy-start(f32[1,128]{1,0:T(1,128)S(1)} %reshape.222.key_gain_ref) | copy-start | bytes 1540
  181.7 18.1 %copy-start.4 = (s32[512,1]{1,0:T(8,128)}, s32[512,1]{1,0:T(8,128)S(1)}, u32[]{:S(2)}) copy-start(s32[512,1]{1,0:T(8,128)S(1)} %copy.53.column_ref) | copy-start | bytes 6148
  181.7 17.8 %copy-start.26 = (f32[512,64]{1,0:T(8,128)S(1)}, f32[512,64]{1,0:T(8,128)}, u32[]{:S(2)}) copy-start(f32[512,64]{1,0:T(8,128)} %get-tuple-element.196) | copy-start | bytes 393220
  199.7 34.9 %copy-start.2 = (f32[512,128]{1,0:T(8,128)}, f32[512,128]{1,0:T(8,128)S(1)}, u32[]{:S(2)}) copy-start(f32[512,128]{1,0:T(8,128)S(1)} %get-tuple-element.203.cosine_ref) | copy-start | bytes 786436
  199.7 34.9 %copy-start.3 = (f32[512,128]{1,0:T(8,128)}, f32[512,128]{1,0:T(8,128)S(1)}, u32[]{:S(2)}) copy-start(f32[512,128]{1,0:T(8,128)S(1)} %get-tuple-element.204.sine_ref) | copy-start | bytes 786436
  234.6 16.2 %copy-start.5 = (f32[4,512,8]{2,1,0:T(8,128)}, f32[4,512,8]{2,1,0:T(8,128)S(1)}, u32[]{:S(2)}) copy-start(f32[4,512,8]{2,1,0:T(8,128)S(1)} %get-tuple-element.87.total_ref) | copy-start | bytes 196612
  234.6 16.2 %copy-start.6 = (bf16[512,512]{1,0:T(8,128)(2,1)}, bf16[512,512]{1,0:T(8,128)(2,1)S(1)}, u32[]{:S(2)}) copy-start(bf16[512,512]{1,0:T(8,128)(2,1)S(1)} %get-tuple-element.83.key_rot_ref) | copy-start | bytes 1572868
  234.6 16.2 %copy-start.7 = (bf16[512,512]{1,0:T(8,128)(2,1)}, bf16[512,512]{1,0:T(8,128)(2,1)S(1)}, u32[]{:S(2)}) copy-start(bf16[512,512]{1,0:T(8,128)(2,1)S(1)} %get-tuple-element.84.value_ref) | copy-start | bytes 1572868
  234.6 16.2 %slice-start.2 = ((bf16[4,18432]{1,0:T(4,128)(2,1)}), bf16[4,16384]{1,0:T(4,128)(2,1)S(1)}, s32[]{:S(2)}) async-start(bf16[4,18432]{1,0:T(4,128)(2,1)} %copy-done.29), calls=%async_computation.8 | async-start | bytes 262144 | tf_op jit(solution)/shard_map/slice | solution.py:1900
  254.5 627.1 %copy-start.21 = (f32[512,32]{0,1:T(8,128)}, f32[512,32]{0,1:T(8,128)S(1)}, u32[]{:S(2)}) copy-start(f32[512,32]{0,1:T(8,128)S(1)} %get-tuple-element.200) | copy-start | bytes 196612
  254.5 627.1 %copy-start.35 = (f32[512]{0:T(512)}, f32[512]{0:T(512)S(1)}, u32[]{:S(2)}) copy-start(f32[512]{0:T(512)S(1)} %get-tuple-element.199) | copy-start | bytes 6148
  254.6 627.1 %copy-start.37 = (f32[512]{0:T(512)}, f32[512]{0:T(512)S(1)}, u32[]{:S(2)}) copy-start(f32[512]{0:T(512)S(1)} %fusion.38) | copy-start | bytes 6148
  254.6 627.0 %copy-start.27 = (pred[512,32]{0,1:T(8,128)(4,1)}, pred[512,32]{0,1:T(8,128)(4,1)S(1)}, u32[]{:S(2)}) copy-start(pred[512,32]{0,1:T(8,128)(4,1)S(1)} %fusion.28) | copy-start | bytes 49156
  254.7 627.0 %copy-start.39 = (f32[512]{0:T(512)}, f32[512]{0:T(512)S(1)}, u32[]{:S(2)}) copy-start(f32[512]{0:T(512)S(1)} %fusion.41) | copy-start | bytes 6148
  870.3 11.2 copy-start.24
  870.3 140.2 %all-to-all-start = ((bf16[8,4,160,1152]{3,2,1,0:T(8,128)(2,1)}), bf16[8,4,160,1152]{3,2,1,0:T(8,128)(2,1)}, u32[]{:S(2)}, u32[]{:S(2)}) async-start(bf16[8,4,160,1152]{3,2,1,0:T(8,128)(2,1)} %bitcast.110), calls=%async_computation | async-start | bytes 23592960 | tf_op jit(solution)/shard_map/all_to_all | solution.py:2017
  881.5 7.7 copy-start.43
  881.7 7.6 copy-start.47
  881.7 7.6 copy-start.12
  881.7 7.6 copy-start.17
  881.7 7.8 copy-start.18
  893.2 15.4 %copy-start.15 = (f32[512,2048]{1,0:T(8,128)}, f32[512,2048]{1,0:T(8,128)S(1)}, u32[]{:S(2)}) copy-start(f32[512,2048]{1,0:T(8,128)S(1)} %fusion.12) | copy-start | bytes 12582916
  908.6 69.6 %slice-start.3 = ((s8[7864320]{0:T(1024)(128)(4,1)}), s8[3670016]{0:T(1024)(128)(4,1)S(1)}, s32[]{:S(2)}) async-start(s8[7864320]{0:T(1024)(128)(4,1)} %bitcast.127), calls=%async_computation.9 | async-start | bytes 7340032
  954.5 23.8 %slice-start.4 = ((s8[7864320]{0:T(1024)(128)(4,1)}), s8[4194304]{0:T(1024)(128)(4,1)S(1)}, s32[]{:S(2)}) async-start(s8[7864320]{0:T(1024)(128)(4,1)} %bitcast.127), calls=%async_computation.10 | async-start | bytes 8388608
  1015.2 107.6 %all-to-all-start.1 = ((bf16[8,4,160,896]{3,2,1,0:T(8,128)(2,1)}), bf16[8,4,160,896]{3,2,1,0:T(8,128)(2,1)}, u32[]{:S(2)}, u32[]{:S(2)}) async-start(bf16[8,4,160,896]{3,2,1,0:T(8,128)(2,1)} %bitcast.111), calls=%async_computation.2 | async-start | bytes 18350080 | tf_op jit(solution)/shard_map/all_to_all | solution.py:2017
  1021.8 349.6 %reduce-scatter.3.cloned.1.call-start = ((), (), s32[]{:S(2)}) async-start(), calls=%async_computation.4 | async-start | bytes 5898240 | tf_op jit(solution)/shard_map/reduce_scatter | solution.py:2034
  1035.0 336.4 %reduce-scatter.5.cloned.1.call-start = ((), (), s32[]{:S(2)}) async-start(), calls=%async_computation.5 | async-start | bytes 4587520 | tf_op jit(solution)/shard_map/reduce_scatter | solution.py:2034
  1037.6 19.6 %copy-start.46 = (f32[512]{0:T(512)S(1)}, f32[512]{0:T(512)}, u32[]{:S(2)}) copy-start(f32[512]{0:T(512)} %copy-done.45) | copy-start | bytes 6148
  1063.2 18.3 %copy-start.16 = (f32[512,2048]{1,0:T(8,128)S(1)}, f32[512,2048]{1,0:T(8,128)}, u32[]{:S(2)}) copy-start(f32[512,2048]{1,0:T(8,128)} %copy-done.15) | copy-start | bytes 12582916
  1119.5 14.3 %copy-start.14 = (bf16[512,2048]{1,0:T(8,128)(2,1)S(1)}, bf16[512,2048]{1,0:T(8,128)(2,1)}, u32[]{:S(2)}) copy-start(bf16[512,2048]{1,0:T(8,128)(2,1)} %copy-done.13) | copy-start | bytes 6291460
  1119.5 14.3 %copy-start.22 = (f32[512,32]{0,1:T(8,128)S(1)}, f32[512,32]{0,1:T(8,128)}, u32[]{:S(2)}) copy-start(f32[512,32]{0,1:T(8,128)} %copy-done.21) | copy-start | bytes 196612
  1119.5 14.3 %copy-start.25 = (f32[4,8,1,512]{3,2,1,0:T(1,128)S(1)}, f32[4,8,1,512]{3,2,1,0:T(1,128)}, u32[]{:S(2)}) copy-start(f32[4,8,1,512]{3,2,1,0:T(1,128)} %get-tuple-element.86) | copy-start | bytes 196612
  1119.5 14.3 %copy-start.28 = (pred[512,32]{0,1:T(8,128)(4,1)S(1)}, pred[512,32]{0,1:T(8,128)(4,1)}, u32[]{:S(2)}) copy-start(pred[512,32]{0,1:T(8,128)(4,1)} %copy-done.27) | copy-start | bytes 49156
  1119.5 14.3 %copy-start.36 = (f32[512]{0:T(512)S(1)}, f32[512]{0:T(512)}, u32[]{:S(2)}) copy-start(f32[512]{0:T(512)} %copy-done.35) | copy-start | bytes 6148
  1119.5 14.3 %copy-start.38 = (f32[512]{0:T(512)S(1)}, f32[512]{0:T(512)}, u32[]{:S(2)}) copy-start(f32[512]{0:T(512)} %copy-done.37) | copy-start | bytes 6148
  1119.5 14.3 %copy-start.40 = (f32[512]{0:T(512)S(1)}, f32[512]{0:T(512)}, u32[]{:S(2)}) copy-start(f32[512]{0:T(512)} %copy-done.39) | copy-start | bytes 6148
  1119.6 14.3 %copy-start.44 = (f32[512]{0:T(512)S(1)}, f32[512]{0:T(512)}, u32[]{:S(2)}) copy-start(f32[512]{0:T(512)} %copy-done.43) | copy-start | bytes 6148
  1119.6 14.3 %copy-start.48 = (f32[512]{0:T(512)S(1)}, f32[512]{0:T(512)}, u32[]{:S(2)}) copy-start(f32[512]{0:T(512)} %copy-done.47) | copy-start | bytes 6148
  1355.2 6.8 slice-start
  1355.2 6.8 slice-start.1
  (16 other events, 41.6 us)
Sparse Core Ops, SparseCore 0:
  1035.1 84.0 reduce-scatter.2
  1133.9 77.2 reduce-scatter.4
